TPU v7x, 32 devices: a whole 2x2x4 slice. The times are simulated.
32 devices in a mesh: segment: 2 (over core), dp: 8 (over z, y), tensor: 2 (over x).
Axes of the slice: x: 2, y: 2, z: 4, core: 2. Of those that a mesh axis runs over, the one named last changes fastest.
Arguments:
- layer_input: bfloat16 [2, 8, 128, 768], P(None, 'dp'), may hold values from -8 to 8
- doc_lengths: int32 [2, 8, 3], P(None, 'dp'), may hold values from 1 to 4, 8 in all within a row
- norm_gains: float32 [2, 2, 768], P('segment'), may hold values from 0.5 to 1.5
- mixing: bfloat16 [2, 768, 4, 768], P('segment', None, None, 'tensor'), may hold values from -0.21875 to 0.21875
- rate_weight: bfloat16 [2, 768, 12], P('segment', None, 'tensor'), may hold values from -0.21875 to 0.21875
- rate_offset: float32 [2, 12], P('segment', 'tensor'), may hold values from -1 to 1
- expand: float32 [2, 12, 64, 256], P('segment', 'tensor'), may hold values from -0.75 to 0.75
- hidden_bias: float32 [2, 12, 256], P('segment', 'tensor'), may hold values from -3 to 3
- contract: float32 [2, 12, 256, 64], P('segment', 'tensor'), may hold values from -0.375 to 0.375
- result_bias: float32 [2, 12, 64], P('segment', 'tensor'), may hold values from -3 to 3
- head_gains: float32 [2, 2, 12, 64], P('segment', None, 'tensor'), may hold values from 0.5 to 1.5
- head_shift: float32 [2, 12, 64], P('segment', 'tensor'), may hold values from -2 to 2
- output_proj: bfloat16 [2, 768, 768], P('segment', 'tensor'), may hold values from -0.4375 to 0.4375
- swiglu: bfloat16 [2, 768, 2, 2048], P('segment', None, None, 'tensor'), may hold values from -0.21875 to 0.21875
- down_proj: bfloat16 [2, 2048, 768], P('segment', 'tensor'), may hold values from -0.25 to 0.25
- cotangent: bfloat16 [2, 8, 128, 768], P(None, 'dp'), may hold values from -6 to 6
Outputs:
- layer_output: bfloat16 [2, 2, 8, 128, 768], P('segment', None, 'dp')
- input_grads: float32 [2, 2, 8, 128, 768], P('segment', None, 'dp')
- grad_gains: float32 [2, 2, 768], P('segment')
- grad_mixing: float32 [2, 768, 4, 768], P('segment', None, None, 'tensor')
- grad_rate: float32 [2, 768, 12], P('segment', None, 'tensor')
- grad_offset: float32 [2, 12], P('segment', 'tensor')
- grad_expand: float32 [2, 12, 64, 256], P('segment', 'tensor')
- grad_hidden: float32 [2, 12, 256], P('segment', 'tensor')
- grad_contract: float32 [2, 12, 256, 64], P('segment', 'tensor')
- grad_result: float32 [2, 12, 64], P('segment', 'tensor')
- grad_heads: float32 [2, 2, 12, 64], P('segment', None, 'tensor')
- grad_shift: float32 [2, 12, 64], P('segment', 'tensor')
- grad_output: float32 [2, 768, 768], P('segment', 'tensor')
- grad_swiglu: float32 [2, 768, 2, 2048], P('segment', None, None, 'tensor')
- grad_down: float32 [2, 2048, 768], P('segment', 'tensor')
- rate_stats: float32 [2, 2, 8, 2, 12], P('segment')
Inputs may be any that keep to these rules, and one draw needn't show every extreme that they name: `doc_lengths`: lengths are counted in inner blocks of 16 tokens; the 3 lengths of a row sum to 8, and in every row the longest is exactly 4.
All inputs are finite; a program needn't handle non-finite values.
Results may differ from a plain program's by a relative error of at most 0.023.
Values may be sent and summed in bfloat16 or wider, within the bound.
No kernel may reach another device: no remote copies, remote signals or barrier semaphores. Data moves between devices by JAX's collectives and lax.ppermute only.
A program may use at most 192 MiB of HBM per device.

v0:
```python
import jax
import jax.numpy as jnp
from jax import lax
from jax.sharding import PartitionSpec as P

MBT = 16


epsilon = 1e-06
rate_scale = 0.125
highest = lax.Precision.HIGHEST
slope_const = 0.7978845608028654


def from_behind(value, axis, by):
    count = lax.axis_size(axis)
    pairs = [(i, i + by) for i in range(count) if 0 <= i + by < count]
    return lax.ppermute(value, axis, pairs)


def exact_dot(left, right):
    return jnp.dot(left, right, precision=highest)


def rms_scale(values, gain):
    return values * lax.rsqrt(jnp.mean(values * values, axis=-1, keepdims=True) + epsilon) * gain


def center_scale(values, gain, shift_in):
    centered = values - jnp.mean(values, axis=-1, keepdims=True)
    return (
        centered * lax.rsqrt(jnp.mean(centered * centered, axis=-1, keepdims=True) + epsilon) * gain
        + shift_in
    )


def gelu_tanh(point):
    return jax.nn.gelu(point, approximate=True)


def gelu_slope(point):
    tangent = jnp.tanh(slope_const * (point + 0.044715 * point * point * point))
    return 0.5 * (1.0 + tangent) + 0.5 * point * (1.0 - tangent * tangent) * slope_const * (
        1.0 + 0.134145 * point * point
    )


def ttt_head(
    queries, keys_in, values_in, rates, resets, first_w, first_b, second_w, second_b, gain, shift_in
):
    blocks = resets.shape[0]
    block_len = queries.shape[0] // blocks
    positions = jnp.arange(block_len)
    causal = (positions[:, None] >= positions[None, :]).astype(jnp.float32)
    weighting = causal / (positions[:, None] + 1).astype(jnp.float32)
    initial = (first_w, first_b, second_w, second_b)

    def block_update(state, inputs):
        query_blk, key_blk, value_blk, rate_blk, flag = inputs
        state = jax.tree.map(lambda now, start: flag * start + (1.0 - flag) * now, state, initial)
        up_w, up_b, down_w, down_b = state
        pre_one = exact_dot(key_blk, up_w) + up_b
        act_one = gelu_tanh(pre_one)
        pre_two = exact_dot(act_one, down_w) + down_b
        centered = pre_two - jnp.mean(pre_two, axis=-1, keepdims=True)
        inv_std = lax.rsqrt(jnp.mean(centered * centered, axis=-1, keepdims=True) + epsilon)
        normed = centered * inv_std
        misfit = (normed * gain + shift_in - (value_blk - key_blk)) * gain
        grad_two = (
            misfit
            - jnp.mean(misfit, axis=-1, keepdims=True)
            - normed * jnp.mean(misfit * normed, axis=-1, keepdims=True)
        ) * inv_std
        grad_one = exact_dot(grad_two, down_w.T) * gelu_slope(pre_one)
        coeff = weighting * rate_blk[None, :]
        new_one = (
            exact_dot(query_blk, up_w)
            + up_b
            - exact_dot(coeff * (exact_dot(query_blk, key_blk.T) + 1.0), grad_one)
        )
        new_act = gelu_tanh(new_one)
        new_two = (
            exact_dot(new_act, down_w)
            + down_b
            - exact_dot(coeff * (exact_dot(new_act, act_one.T) + 1.0), grad_two)
        )
        out_blk = query_blk + center_scale(new_two, gain, shift_in)
        last_rate = (rate_blk / block_len)[:, None]
        step_one = last_rate * grad_one
        step_two = last_rate * grad_two
        state = (
            up_w - exact_dot(key_blk.T, step_one),
            up_b - jnp.sum(step_one, axis=0),
            down_w - exact_dot(act_one.T, step_two),
            down_b - jnp.sum(step_two, axis=0),
        )
        return (state, out_blk)

    def to_blocks(array):
        return array.reshape((blocks, block_len) + array.shape[1:])

    _, outputs = lax.scan(
        jax.checkpoint(block_update),
        initial,
        (to_blocks(queries), to_blocks(keys_in), to_blocks(values_in), to_blocks(rates), resets),
    )
    return outputs.reshape(queries.shape)


def mixer(projected, logits, resets, first_w, first_b, second_w, second_b, gains_in, shift_in):
    row_count, length, _, width_all = projected.shape
    head_count = logits.shape[-1]
    sections = projected.reshape(row_count, length, 4, head_count, width_all // head_count)
    rates = jax.nn.sigmoid(logits) * rate_scale
    per_head = jax.vmap(ttt_head, in_axes=(1, 1, 1, 1, None, 0, 0, 0, 0, 0, 0), out_axes=1)
    per_row = jax.vmap(per_head, in_axes=(0, 0, 0, 0, 0, None, None, None, None, None, None))
    inner_out = per_row(
        sections[:, :, 0],
        sections[:, :, 1],
        sections[:, :, 2],
        rates,
        resets,
        first_w,
        first_b,
        second_w,
        second_b,
        gains_in[0],
        shift_in,
    )
    mixed = gelu_tanh(sections[:, :, 3]) * rms_scale(inner_out, gains_in[1])
    return mixed.reshape(row_count, length, width_all)


def rate_summary(logits):
    probs = jax.nn.sigmoid(logits)
    return jnp.stack([jnp.mean(probs, axis=1), jnp.max(probs, axis=1)], axis=1)


def reset_flags(lengths, blocks):
    starts = jnp.cumsum(lengths, axis=-1) - lengths
    marks = jnp.arange(blocks, dtype=jnp.int32)
    hits = (starts[..., :, None] == marks).astype(jnp.float32)
    return jnp.sum(hits, axis=-2)


def gated_unit(gate_pre):
    half_width = gate_pre.shape[-1] // 2
    return jax.nn.silu(gate_pre[:, :half_width]) * gate_pre[:, half_width:]


def flatten_all(parts):
    return jnp.concatenate([jnp.ravel(part) for part in parts])


def restore(vector, likes):
    pieces = []
    offset_at = 0
    for like in likes:
        count = like.size
        pieces.append(vector[offset_at : offset_at + count].reshape(like.shape))
        offset_at = offset_at + count
    return tuple(pieces)


def shards(
    layer_input,
    doc_lengths,
    norm_gains,
    mixing,
    rate_weight,
    rate_offset,
    expand,
    hidden_bias,
    contract,
    result_bias,
    head_gains,
    head_shift,
    output_proj,
    swiglu,
    down_proj,
    cotangent,
):
    micro_count, row_count, length, model_width = layer_input.shape
    first_segment = lax.axis_index("segment") == 0
    gain_pair = norm_gains[0]
    mix_mat = mixing[0].reshape(model_width, -1)
    rate_mat = rate_weight[0]
    offset_row = rate_offset[0]
    inner_params = (
        expand[0],
        hidden_bias[0],
        contract[0],
        result_bias[0],
        head_gains[0],
        head_shift[0],
    )
    out_mat = output_proj[0]
    wide_mat = swiglu[0].reshape(model_width, -1)
    down_mat = down_proj[0]
    flags = reset_flags(doc_lengths, length // MBT)
    param_likes = (
        norm_gains,
        mixing,
        rate_weight,
        rate_offset,
        expand,
        hidden_bias,
        contract,
        result_bias,
        head_gains,
        head_shift,
        output_proj,
        swiglu,
        down_proj,
    )

    def forward(source, resets):
        rows_flat = source.reshape(-1, model_width)
        x_one = rms_scale(rows_flat, gain_pair[0]).astype(jnp.bfloat16)
        projected = jnp.dot(x_one, mix_mat, preferred_element_type=jnp.float32)
        logits = jnp.dot(x_one, rate_mat, preferred_element_type=jnp.float32) + offset_row

        def local_mix(proj_in, logit_in, params_in):
            mixed_all = mixer(
                proj_in.reshape(row_count, length, 4, -1),
                logit_in.reshape(row_count, length, -1),
                resets,
                *params_in
            )
            return mixed_all.reshape(proj_in.shape[0], -1)

        mixed, mix_back = jax.vjp(local_mix, projected, logits, inner_params)
        mixed_low = mixed.astype(jnp.bfloat16)
        mixer_out = lax.psum(
            jnp.dot(mixed_low, out_mat, preferred_element_type=jnp.float32), "tensor"
        )
        h_one = rows_flat + mixer_out
        x_two = rms_scale(h_one, gain_pair[1]).astype(jnp.bfloat16)
        gate_pre = jnp.dot(x_two, wide_mat, preferred_element_type=jnp.float32)
        hidden = gated_unit(gate_pre).astype(jnp.bfloat16)
        feed_out = lax.psum(jnp.dot(hidden, down_mat, preferred_element_type=jnp.float32), "tensor")
        saved = (rows_flat, x_one, mix_back, mixed_low, h_one, x_two, gate_pre, hidden)
        return (h_one + feed_out, saved, rate_summary(logits.reshape(row_count, length, -1)))

    received = jnp.zeros((row_count, length, model_width), jnp.bfloat16)
    outputs = []
    inputs_seen = []
    stores = []
    summaries = []
    for turn_index in range(micro_count + 1):
        own_rows = layer_input[min(turn_index, micro_count - 1)]
        source = jnp.where(first_segment, own_rows, received).astype(jnp.float32)
        resets = jnp.where(
            first_segment, flags[min(turn_index, micro_count - 1)], flags[max(turn_index - 1, 0)]
        )
        result, saved, summary = forward(source, resets)
        result_low = result.reshape(row_count, length, model_width).astype(jnp.bfloat16)
        received = from_behind(result_low, "segment", 1)
        outputs.append(result_low)
        inputs_seen.append((source, resets))
        summaries.append(summary)
        stores.append(saved)
    inbound = jnp.zeros((row_count, length, model_width), jnp.bfloat16)
    totals = None
    grads_in = []
    for turn_index in range(micro_count + 1):
        forward_index = micro_count - turn_index
        own_grad = cotangent[max(micro_count - 1 - turn_index, 0)].astype(jnp.float32)
        grad_out = jnp.where(first_segment, inbound.astype(jnp.float32), own_grad).reshape(
            -1, model_width
        )
        saved = stores[forward_index]
        (
            backward_rows_flat,
            backward_x_one,
            backward_mix_back,
            backward_mixed_low,
            backward_h_one,
            backward_x_two,
            backward_gate_pre,
            backward_hidden,
        ) = saved
        feed_low = grad_out.astype(jnp.bfloat16)
        down_grad = jnp.dot(backward_hidden.T, feed_low, preferred_element_type=jnp.float32)
        hidden_grad = jnp.dot(feed_low, down_mat.T, preferred_element_type=jnp.float32)
        _, unit_back = jax.vjp(gated_unit, backward_gate_pre)
        gate_low = unit_back(hidden_grad)[0].astype(jnp.bfloat16)
        wide_grad = jnp.dot(backward_x_two.T, gate_low, preferred_element_type=jnp.float32)
        x_two_grad = lax.psum(
            jnp.dot(gate_low, wide_mat.T, preferred_element_type=jnp.float32).astype(jnp.bfloat16),
            "tensor",
        ).astype(jnp.float32)
        _, second_back = jax.vjp(rms_scale, backward_h_one, gain_pair[1])
        h_norm_grad, gain_two_grad = second_back(x_two_grad)
        h_one_grad = grad_out + h_norm_grad
        mixer_low = h_one_grad.astype(jnp.bfloat16)
        out_grad = jnp.dot(backward_mixed_low.T, mixer_low, preferred_element_type=jnp.float32)
        mixed_grad = jnp.dot(mixer_low, out_mat.T, preferred_element_type=jnp.float32)
        proj_grad, logit_grad, inner_grad = backward_mix_back(mixed_grad)
        proj_low = proj_grad.astype(jnp.bfloat16)
        logit_low = logit_grad.astype(jnp.bfloat16)
        mix_grad = jnp.dot(backward_x_one.T, proj_low, preferred_element_type=jnp.float32)
        rate_grad = jnp.dot(backward_x_one.T, logit_low, preferred_element_type=jnp.float32)
        x_one_grad = lax.psum(
            (
                jnp.dot(proj_low, mix_mat.T, preferred_element_type=jnp.float32)
                + jnp.dot(logit_low, rate_mat.T, preferred_element_type=jnp.float32)
            ).astype(jnp.bfloat16),
            "tensor",
        ).astype(jnp.float32)
        _, first_back = jax.vjp(rms_scale, backward_rows_flat, gain_pair[0])
        flat_grad, gain_one_grad = first_back(x_one_grad)
        weight_grads = (
            (
                jnp.stack([gain_one_grad, gain_two_grad]),
                mix_grad,
                rate_grad,
                jnp.sum(logit_grad, axis=0),
            )
            + tuple(inner_grad)
            + (out_grad, wide_grad, down_grad)
        )
        input_grad, weight_grads = (h_one_grad + flat_grad, weight_grads)
        is_live = jnp.where(first_segment, turn_index >= 1, turn_index < micro_count)
        weight_grads = jax.tree.map(lambda term: jnp.where(is_live, term, 0.0), weight_grads)
        totals = weight_grads if totals is None else jax.tree.map(jnp.add, totals, weight_grads)
        input_rows = input_grad.reshape(row_count, length, model_width)
        inbound = from_behind(input_rows.astype(jnp.bfloat16), "segment", -1)
        grads_in.append(input_rows)
    totals = restore(lax.psum(flatten_all(totals), "dp"), totals)
    finals = [total.reshape(like.shape) for total, like in zip(totals, param_likes)]
    layer_output = jnp.stack(
        [
            jnp.where(first_segment, outputs[index], outputs[index + 1])
            for index in range(micro_count)
        ]
    )[None]
    input_grads = jnp.stack(
        [
            jnp.where(
                first_segment, grads_in[micro_count - index], grads_in[micro_count - 1 - index]
            )
            for index in range(micro_count)
        ]
    )[None]
    local_stats = jnp.stack(
        [
            jnp.where(first_segment, summaries[index], summaries[index + 1])
            for index in range(micro_count)
        ]
    )
    stats_heads = lax.all_gather(local_stats, "tensor", axis=3, tiled=True)
    rate_stats = lax.all_gather(stats_heads, "dp", axis=1, tiled=True)[None]
    return (
        layer_output,
        input_grads,
        finals[0],
        finals[1],
        finals[2],
        finals[3],
        finals[4],
        finals[5],
        finals[6],
        finals[7],
        finals[8],
        finals[9],
        finals[10],
        finals[11],
        finals[12],
        rate_stats,
    )


def solution(mesh):
    placed = (
        P(None, "dp", None, None),
        P(None, "dp", None),
        P("segment", None, None),
        P("segment", None, None, "tensor"),
        P("segment", None, "tensor"),
        P("segment", "tensor"),
        P("segment", "tensor", None, None),
        P("segment", "tensor", None),
        P("segment", "tensor", None, None),
        P("segment", "tensor", None),
        P("segment", None, "tensor", None),
        P("segment", "tensor", None),
        P("segment", "tensor", None),
        P("segment", None, None, "tensor"),
        P("segment", "tensor", None),
        P(None, "dp", None, None),
    )
    return jax.shard_map(
        shards,
        mesh=mesh,
        in_specs=placed,
        out_specs=(
            P("segment", None, "dp", None, None),
            P("segment", None, "dp", None, None),
            P("segment", None, None),
            P("segment", None, None, "tensor"),
            P("segment", None, "tensor"),
            P("segment", "tensor"),
            P("segment", "tensor", None, None),
            P("segment", "tensor", None),
            P("segment", "tensor", None, None),
            P("segment", "tensor", None),
            P("segment", None, "tensor", None),
            P("segment", "tensor", None),
            P("segment", "tensor", None),
            P("segment", None, None, "tensor"),
            P("segment", "tensor", None),
            P("segment", None, None, None, None),
        ),
        check_vma=False,
    )
```

profile of v0, /device:TPU:0, one launch (start us, length us, event | category | flops | bytes accessed | tf_op | source)
XLA Modules:
  0.0 2588.0 jit_solution(1794194113427369417)
XLA Ops:
  12.6 3.5 copy.460
  16.1 4.3 copy.325
  20.7 2.5 convolution_bitcast_fusion.62
  32.1 2.0 broadcast.3356.clone
  34.8 2.0 broadcast.3358.clone
  37.4 174.8 %while.210 = (s32[]{:T(128)}, f32[1,6,64,256]{3,2,1,0:T(8,128)S(1)}, f32[1,6,256]{2,1,0:T(8,128)S(1)}, f32[1,6,256,64]{2,3,1,0:T(8,128)S(1)}, f32[1,6,64]{2,1,0:...) while((s32[]{:T(128)}, f32[1,6,64,256]{3,2,1,0:T(8,128)S(1)}, ...), condition=%wide.region_12.13_spmd.clone, body=%wide.region_3.12_spmd.clone.sunk | while | flops 146316576 | bytes 9658237 | solution.py:102
  214.5 2.1 fusion.719
  216.8 4.6 copy.461
  221.5 23.8 all-reduce.38.cloned.1.call-done
  247.2 2.5 fusion.939
  252.9 25.7 all-reduce.40.cloned.1.call-done
  279.8 2.0 collective-permute-start
  284.2 2.5 convolution_bitcast_fusion.61
  300.9 2.0 broadcast.3356.clone.1
  303.6 2.0 broadcast.3358.clone.1
  306.2 174.9 %while.211 = (s32[]{:T(128)}, f32[1,6,64,256]{3,2,1,0:T(8,128)S(1)}, f32[1,6,256]{2,1,0:T(8,128)S(1)}, f32[1,6,256,64]{2,3,1,0:T(8,128)S(1)}, f32[1,6,64]{2,1,0:...) while((s32[]{:T(128)}, f32[1,6,64,256]{3,2,1,0:T(8,128)S(1)}, ...), condition=%wide.region_27.28_spmd.clone, body=%wide.region_18.27_spmd.clone.sunk | while | flops 146316576 | bytes 9658237 | solution.py:102
  483.4 2.1 fusion.717
  485.7 25.9 all-reduce.42.cloned.1.call-done
  512.7 2.7 fusion.940
  517.8 25.8 all-reduce.44.cloned.1.call-done
  545.4 2.8 collective-permute-start.1
  549.9 2.5 convolution_bitcast_fusion.60
  566.6 2.1 broadcast.3356
  569.3 2.1 broadcast.3358
  572.0 175.0 %while.212 = (s32[]{:T(128)}, f32[1,6,64,256]{3,2,1,0:T(8,128)S(1)}, f32[1,6,256]{2,1,0:T(8,128)S(1)}, f32[1,6,256,64]{2,3,1,0:T(8,128)S(1)}, f32[1,6,64]{2,1,0:...) while((s32[]{:T(128)}, f32[1,6,64,256]{3,2,1,0:T(8,128)S(1)}, ...), condition=%wide.region_42.43_spmd.clone, body=%wide.region_33.42_spmd.clone.sunk | while | flops 146316576 | bytes 9658237 | solution.py:102
  749.2 2.2 fusion.715
  751.5 26.0 %all-reduce.46.cloned.1.call-done = f32[128,768]{1,0:T(8,128)} async-done(((f32[128,768]{1,0:T(8,128)}), f32[128,768]{1,0:T(8,128)}) %all-reduce.46.cloned.1.call-update) | async-done | bytes 393232 | tf_op jit(solution)/shard_map/psum | solution.py:234
  779.3 2.5 fusion.941
  786.3 22.3 all-reduce.50.cloned.1.call-done
  812.5 2.4 multiply_reduce_fusion.47
  819.9 278.4 %while.213 = (s32[]{:T(128)}, f32[6,64,256]{2,1,0:T(8,128)}, f32[6,256]{1,0:T(8,128)}, f32[6,256,64]{1,2,0:T(8,128)}, f32[6,64]{1,0:T(8,128)}, /*index=5*/f32[6,...) while((s32[]{:T(128)}, f32[6,64,256]{2,1,0:T(8,128)}, ...), condition=%wide.region_76.77_spmd.clone, body=%wide.region_50.76_spmd.clone.sunk | while | flops 402749568 | bytes 31308580 | solution.py:102
  1110.0 3.4 fusion.688
  1113.5 22.4 all-reduce.52.cloned.1.call-done
  1140.2 2.0 collective-permute-done.2
  1142.3 2.0 fusion.880
  1147.3 22.3 all-reduce.54.cloned.1.call-done
  1179.3 288.0 %while.214 = (s32[]{:T(128)}, f32[6,64,256]{2,1,0:T(8,128)}, f32[6,256]{1,0:T(8,128)}, f32[6,256,64]{1,2,0:T(8,128)}, f32[6,64]{1,0:T(8,128)}, /*index=5*/f32[6,...) while((s32[]{:T(128)}, f32[6,64,256]{2,1,0:T(8,128)}, ...), condition=%wide.region_108.109_spmd.clone, body=%wide.region_82.108_spmd.clone.sunk | while | flops 402749568 | bytes 31283948 | solution.py:102
  1479.0 3.3 fusion.689
  1482.4 22.3 all-reduce.56.cloned.1.call-done
  1510.0 5.0 fusion.874
  1519.3 3.3 fusion.824
  1522.7 19.8 all-reduce.58.cloned.1.call-done
  1552.1 276.1 %while.215 = (s32[]{:T(128)}, f32[6,64,256]{2,1,0:T(8,128)}, f32[6,256]{1,0:T(8,128)}, f32[6,256,64]{1,2,0:T(8,128)}, f32[6,64]{1,0:T(8,128)}, /*index=5*/f32[6,...) while((s32[]{:T(128)}, f32[6,64,256]{2,1,0:T(8,128)}, ...), condition=%wide.region_140.141_spmd.clone, body=%wide.region_114.140_spmd.clone.sunk | while | flops 402749568 | bytes 31283948 | solution.py:102
  1836.5 3.3 fusion.690
  1839.9 2.1 fusion.681
  1842.4 3.0 fusion.837
  1849.0 3.3 fusion.843
  1856.9 4.2 copy.463
  1861.1 2.3 select_add_fusion.7
  1863.5 4.4 reshape.5896
  1868.5 5.6 select_add_fusion.6
  1874.1 5.7 reshape.5886
  1892.3 2.6 fusion.687
  1895.0 2.3 reshape.5894
  1899.1 139.3 %concatenate.39 = f32[4039686]{0:T(1024)} concatenate(f32[1536]{0:T(1024)S(1)} %add.2004, f32[1179648]{0:T(1024)} %reshape.5886, f32[4608]{0:T(1024)S(1)} %copy-done.140, f32[6]{0:T(128)S(1)} %fusion.924, f32[98304]{0:T(1024)S(1)} %bitcast.3364, f32[1536]{0:T(1024)S(1)} %reshape.5889, f32[98304]{0:T(1024)S(1)} %copy-done.86, f32[384]{0:T(512)S(1)} %reshape.5891, ...), dimensions={0} | concatenate | bytes 32317488 | tf_op jit(solution)/shard_map/concatenate | solution.py:152
  2041.2 4.3 all_gather.6
  2045.6 23.3 all_gather.7
  2076.5 456.4 %all-reduce.62.cloned.1.call-done = f32[4039686]{0:T(1024)} async-done(((f32[4039686]{0:T(1024)}), f32[4039686]{0:T(1024)}) %all-reduce.62.cloned.1.call-update) | async-done | bytes 16158760 | tf_op jit(solution)/shard_map/psum | solution.py:330
  2534.3 4.0 slice.218
  2538.3 6.5 reshape_reshape.37
  2557.1 5.4 slice.228
  2562.6 8.2 reshape_reshape.46
  2570.8 4.4 slice.229
  2575.2 4.6 reshape_reshape.47
  (4197 shorter events, 1531.7 us)
Async XLA Ops:
  7.2 244.4 %copy-start = (bf16[1,1024,768]{2,1,0:T(8,128)(2,1)S(1)}, bf16[1,1024,768]{2,1,0:T(8,128)(2,1)}, u32[]{:S(2)}) copy-start(bf16[1,1024,768]{2,1,0:T(8,128)(2,1)} %param.42) | copy-start | bytes 4718596
  7.2 238.1 %all-reduce.38.cloned.1.call-start = ((), (), s32[]{:S(2)}) async-start(), calls=%async_computation | async-start | bytes 786432 | tf_op jit(solution)/shard_map/psum | solution.py:234
  37.4 176.0 %copy-start.176 = (f32[1,1,6,64]{3,1,2,0:T(1,128)S(1)}, f32[1,1,6,64]{3,1,2,0:T(1,128)}, u32[]{:S(2)}) copy-start(f32[1,1,6,64]{3,1,2,0:T(1,128)} %get-tuple-element.4463) | copy-start | bytes 4612
  216.7 61.9 %all-reduce.40.cloned.1.call-start = ((), (), s32[]{:S(2)}) async-start(), calls=%async_computation.1 | async-start | bytes 786432 | tf_op jit(solution)/shard_map/psum | solution.py:241
  216.8 28.5 %copy-start.44 = (bf16[2,1,128,768]{3,2,1,0:T(8,128)(2,1)S(1)}, bf16[2,1,128,768]{3,2,1,0:T(8,128)(2,1)}, u32[]{:S(2)}) copy-start(bf16[2,1,128,768]{3,2,1,0:T(8,128)(2,1)} %param.28) | copy-start | bytes 1179652
  250.7 31.0 %copy-start.178 = (f32[2,8]{1,0:T(2,128)S(1)}, f32[2,8]{1,0:T(2,128)}, u32[]{:S(2)}) copy-start(f32[2,8]{1,0:T(2,128)} %copy-done.177) | copy-start | bytes 196
  252.7 258.8 %all-reduce.42.cloned.1.call-start = ((), (), s32[]{:S(2)}) async-start(), calls=%async_computation.2 | async-start | bytes 786432 | tf_op jit(solution)/shard_map/psum | solution.py:234
  252.8 33.9 %copy-start.211 = (f32[1,6]{1,0:T(1,128)S(1)}, f32[1,6]{1,0:T(1,128)}, u32[]{:S(2)}) copy-start(f32[1,6]{1,0:T(1,128)} %param.33) | copy-start | bytes 76
  279.8 2.8 collective-permute-start
  283.7 227.9 %copy-start.40 = (bf16[1,128,768]{2,1,0:T(8,128)(2,1)}, bf16[1,128,768]{2,1,0:T(8,128)(2,1)S(1)}, u32[]{:S(2)}) copy-start(bf16[1,128,768]{2,1,0:T(8,128)(2,1)S(1)} %get-tuple-element.4341) | copy-start | bytes 589828
  481.1 34.3 %copy-start.135 = (f32[8,1,6,16]{3,0,1,2:T(8,128)}, f32[8,1,6,16]{3,0,1,2:T(8,128)S(1)}, u32[]{:S(2)}) copy-start(f32[8,1,6,16]{3,0,1,2:T(8,128)S(1)} %get-tuple-element.6554) | copy-start | bytes 9220
  481.1 34.3 %copy-start.150 = (f32[8,1]{0,1:T(1,128)}, f32[8,1]{0,1:T(1,128)S(1)}, u32[]{:S(2)}) copy-start(f32[8,1]{0,1:T(1,128)S(1)} %get-tuple-element.6557) | copy-start | bytes 100
  482.3 33.1 %copy-start.147 = (f32[128,6]{0,1:T(8,128)}, f32[128,6]{0,1:T(8,128)S(1)}, u32[]{:S(2)}) copy-start(f32[128,6]{0,1:T(8,128)S(1)} %fusion.841) | copy-start | bytes 9220
  482.3 33.1 %copy-start.143 = (f32[128,6]{0,1:T(8,128)}, f32[128,6]{0,1:T(8,128)S(1)}, u32[]{:S(2)}) copy-start(f32[128,6]{0,1:T(8,128)S(1)} %fusion.908) | copy-start | bytes 9220
  485.6 58.0 %all-reduce.44.cloned.1.call-start = ((), (), s32[]{:S(2)}) async-start(), calls=%async_computation.3 | async-start | bytes 786432 | tf_op jit(solution)/shard_map/psum | solution.py:241
  512.7 30.9 %copy-start.12 = (f32[128,768]{1,0:T(8,128)}, f32[128,768]{1,0:T(8,128)S(1)}, u32[]{:S(2)}) copy-start(f32[128,768]{1,0:T(8,128)S(1)} %get-tuple-element.4339) | copy-start | bytes 1179652
  512.7 30.9 %copy-start.99 = (bf16[128,768]{1,0:T(8,128)(2,1)S(1)}, bf16[128,768]{1,0:T(8,128)(2,1)}, u32[]{:S(2)}) copy-start(bf16[128,768]{1,0:T(8,128)(2,1)} %copy-done.98) | copy-start | bytes 589828
  516.5 31.7 %copy-start.72 = (bf16[128,1024]{1,0:T(8,128)(2,1)}, bf16[128,1024]{1,0:T(8,128)(2,1)S(1)}, u32[]{:S(2)}) copy-start(bf16[128,1024]{1,0:T(8,128)(2,1)S(1)} %multiply_convert_fusion.1) | copy-start | bytes 786436
  517.7 34.7 %copy-start.139 = (bf16[1,768,6]{1,2,0:T(8,128)(2,1)S(1)}, bf16[1,768,6]{1,2,0:T(8,128)(2,1)}, u32[]{:S(2)}) copy-start(bf16[1,768,6]{1,2,0:T(8,128)(2,1)} %param.32) | copy-start | bytes 27652
  517.7 34.7 %copy-start.212 = (f32[1,6]{1,0:T(1,128)S(1)}, f32[1,6]{1,0:T(1,128)}, u32[]{:S(2)}) copy-start(f32[1,6]{1,0:T(1,128)} %param.33) | copy-start | bytes 76
  517.7 259.7 %all-reduce.46.cloned.1.call-start = ((), (), s32[]{:S(2)}) async-start(), calls=%async_computation.4 | async-start | bytes 786432 | tf_op jit(solution)/shard_map/psum | solution.py:234
  545.4 2.9 collective-permute-start.1
  549.4 1296.0 %copy-start.38 = (bf16[1,128,768]{2,1,0:T(8,128)(2,1)}, bf16[1,128,768]{2,1,0:T(8,128)(2,1)S(1)}, u32[]{:S(2)}) copy-start(bf16[1,128,768]{2,1,0:T(8,128)(2,1)S(1)} %get-tuple-element.4337) | copy-start | bytes 589828
  746.9 34.9 %copy-start.151 = (f32[8,1]{0,1:T(1,128)}, f32[8,1]{0,1:T(1,128)S(1)}, u32[]{:S(2)}) copy-start(f32[8,1]{0,1:T(1,128)S(1)} %get-tuple-element.6558) | copy-start | bytes 100
  749.2 32.6 %copy-start.93 = (bf16[1,128,6,64]{1,3,2,0:T(8,128)(2,1)}, bf16[1,128,6,64]{1,3,2,0:T(8,128)(2,1)S(1)}, u32[]{:S(2)}) copy-start(bf16[1,128,6,64]{1,3,2,0:T(8,128)(2,1)S(1)} %multiply_convert_fusion.6) | copy-start | bytes 294916
  751.4 30.5 %copy-start.67 = (bf16[2,1,128,768]{3,2,1,0:T(8,128)(2,1)S(1)}, bf16[2,1,128,768]{3,2,1,0:T(8,128)(2,1)}, u32[]{:S(2)}) copy-start(bf16[2,1,128,768]{3,2,1,0:T(8,128)(2,1)} %param.43) | copy-start | bytes 1179652
  751.4 57.2 %all-reduce.50.cloned.1.call-start = ((), (), s32[]{:S(2)}) async-start(), calls=%async_computation.6 | async-start | bytes 393216 | tf_op jit(solution)/shard_map/psum | solution.py:289
  778.6 31.9 %copy-start.160 = (f32[128]{0:T(128)}, f32[128]{0:T(128)S(1)}, u32[]{:S(2)}) copy-start(f32[128]{0:T(128)S(1)} %fusion.930) | copy-start | bytes 1540
  784.3 27.5 %copy-start.6 = (bf16[1,384,768]{2,1,0:T(8,128)(2,1)S(1)}, bf16[1,384,768]{2,1,0:T(8,128)(2,1)}, u32[]{:S(2)}) copy-start(bf16[1,384,768]{2,1,0:T(8,128)(2,1)} %param.40) | copy-start | bytes 1769476
  786.2 349.7 %all-reduce.52.cloned.1.call-start = ((), (), s32[]{:S(2)}) async-start(), calls=%async_computation.7 | async-start | bytes 393216 | tf_op jit(solution)/shard_map/psum | solution.py:304
  1106.1 29.9 %copy-start.166 = (f32[128]{0:T(128)S(1)}, f32[128]{0:T(128)}, u32[]{:S(2)}) copy-start(f32[128]{0:T(128)} %copy-done.165) | copy-start | bytes 1540
  1106.1 31.6 %copy-start.209 = (f32[128]{0:T(128)S(1)}, f32[128]{0:T(128)}, u32[]{:S(2)}) copy-start(f32[128]{0:T(128)} %copy-done.208) | copy-start | bytes 1540
  1106.1 31.6 %copy-start.35 = (f32[128,768]{1,0:T(8,128)S(1)}, f32[128,768]{1,0:T(8,128)}, u32[]{:S(2)}) copy-start(f32[128,768]{1,0:T(8,128)} %copy-done.34) | copy-start | bytes 1179652
  1110.0 34.3 %copy-start.63 = (bf16[1,128,4,6,64]{1,4,3,2,0:T(8,128)(2,1)}, bf16[1,128,4,6,64]{1,4,3,2,0:T(8,128)(2,1)S(1)}, u32[]{:S(2)}) copy-start(bf16[1,128,4,6,64]{1,4,3,2,0:T(8,128)(2,1)S(1)} %add_convert_fusion.5) | copy-start | bytes 1179652
  1113.4 56.2 %all-reduce.54.cloned.1.call-start = ((), (), s32[]{:S(2)}) async-start(), calls=%async_computation.8 | async-start | bytes 393216 | tf_op jit(solution)/shard_map/psum | solution.py:289
  1138.9 3.3 collective-permute-start.2
  1144.3 25.3 copy-start.163
  1144.3 27.2 %copy-start.202 = (f32[128]{0:T(128)S(1)}, f32[128]{0:T(128)}, u32[]{:S(2)}) copy-start(f32[128]{0:T(128)} %copy-done.201) | copy-start | bytes 1540
  1145.3 27.6 %copy-start.7 = (bf16[1,384,768]{2,1,0:T(8,128)(2,1)S(1)}, bf16[1,384,768]{2,1,0:T(8,128)(2,1)}, u32[]{:S(2)}) copy-start(bf16[1,384,768]{2,1,0:T(8,128)(2,1)} %param.40) | copy-start | bytes 1769476
  1145.3 28.4 %copy-start.59 = (f32[1,6,128,64]{2,3,1,0:T(8,128)S(1)}, f32[1,6,128,64]{2,3,1,0:T(8,128)}, u32[]{:S(2)}) copy-start(f32[1,6,128,64]{2,3,1,0:T(8,128)} %copy-done.58) | copy-start | bytes 589828
  1145.3 28.4 %copy-start.144 = (f32[128,6]{0,1:T(8,128)S(1)}, f32[128,6]{0,1:T(8,128)}, u32[]{:S(2)}) copy-start(f32[128,6]{0,1:T(8,128)} %copy-done.143) | copy-start | bytes 9220
  1147.1 28.1 %copy-start.148 = (f32[128,6]{0,1:T(8,128)S(1)}, f32[128,6]{0,1:T(8,128)}, u32[]{:S(2)}) copy-start(f32[128,6]{0,1:T(8,128)} %copy-done.147) | copy-start | bytes 9220
  1147.2 357.6 %all-reduce.56.cloned.1.call-start = ((), (), s32[]{:S(2)}) async-start(), calls=%async_computation.9 | async-start | bytes 393216 | tf_op jit(solution)/shard_map/psum | solution.py:304
  1475.0 29.8 %copy-start.41 = (bf16[1,128,768]{2,1,0:T(8,128)(2,1)S(1)}, bf16[1,128,768]{2,1,0:T(8,128)(2,1)}, u32[]{:S(2)}) copy-start(bf16[1,128,768]{2,1,0:T(8,128)(2,1)} %copy-done.40) | copy-start | bytes 589828
  1475.0 29.8 %copy-start.191 = (f32[128]{0:T(128)S(1)}, f32[128]{0:T(128)}, u32[]{:S(2)}) copy-start(f32[128]{0:T(128)} %copy-done.190) | copy-start | bytes 1540
  1475.0 31.5 %copy-start.207 = (f32[128]{0:T(128)S(1)}, f32[128]{0:T(128)}, u32[]{:S(2)}) copy-start(f32[128]{0:T(128)} %copy-done.206) | copy-start | bytes 1540
  1476.9 33.1 %copy-start.10 = (f32[128,768]{1,0:T(8,128)S(1)}, f32[128,768]{1,0:T(8,128)}, u32[]{:S(2)}) copy-start(f32[128,768]{1,0:T(8,128)} %copy-done.9) | copy-start | bytes 1179652
  1476.9 33.1 %copy-start.161 = (f32[128]{0:T(128)S(1)}, f32[128]{0:T(128)}, u32[]{:S(2)}) copy-start(f32[128]{0:T(128)} %copy-done.160) | copy-start | bytes 1540
  1482.3 60.2 %all-reduce.58.cloned.1.call-start = ((), (), s32[]{:S(2)}) async-start(), calls=%async_computation.10 | async-start | bytes 393216 | tf_op jit(solution)/shard_map/psum | solution.py:289
  1508.4 6.6 collective-permute-start.3
  1517.4 25.1 copy-start.180
  1519.2 25.2 copy-start.205
  1519.2 26.6 %copy-start.8 = (bf16[1,384,768]{2,1,0:T(8,128)(2,1)S(1)}, bf16[1,384,768]{2,1,0:T(8,128)(2,1)}, u32[]{:S(2)}) copy-start(bf16[1,384,768]{2,1,0:T(8,128)(2,1)} %param.40) | copy-start | bytes 1769476
  1519.2 378.1 %all-reduce.60.cloned.1.call-start = ((), (), s32[]{:S(2)}) async-start(), calls=%async_computation.11 | async-start | bytes 393216 | tf_op jit(solution)/shard_map/psum | solution.py:304
  1519.3 27.2 %copy-start.57 = (f32[1,6,128,64]{2,3,1,0:T(8,128)S(1)}, f32[1,6,128,64]{2,3,1,0:T(8,128)}, u32[]{:S(2)}) copy-start(f32[1,6,128,64]{2,3,1,0:T(8,128)} %copy-done.56) | copy-start | bytes 589828
  1519.3 27.2 %copy-start.142 = (f32[128,6]{0,1:T(8,128)S(1)}, f32[128,6]{0,1:T(8,128)}, u32[]{:S(2)}) copy-start(f32[128,6]{0,1:T(8,128)} %copy-done.141) | copy-start | bytes 9220
  1519.3 28.7 %copy-start.146 = (f32[128,6]{0,1:T(8,128)S(1)}, f32[128,6]{0,1:T(8,128)}, u32[]{:S(2)}) copy-start(f32[128,6]{0,1:T(8,128)} %copy-done.145) | copy-start | bytes 9220
  1839.9 230.8 %all-reduce.48.cloned.1.call-start = ((), (), s32[]{:S(2)}) async-start(), calls=%async_computation.5 | async-start | bytes 786432 | tf_op jit(solution)/shard_map/psum | solution.py:241
  1842.1 690.9 %all-reduce.62.cloned.1.call-start = ((), (), s32[]{:S(2)}) async-start(), calls=%async_computation.12 | async-start | bytes 32325632 | tf_op jit(solution)/shard_map/psum | solution.py:330
  2038.4 32.2 %copy-start.11 = (f32[128,768]{1,0:T(8,128)S(1)}, f32[128,768]{1,0:T(8,128)}, u32[]{:S(2)}) copy-start(f32[128,768]{1,0:T(8,128)} %copy-done.9) | copy-start | bytes 1179652
  2038.4 35.8 %copy-start.37 = (f32[128,768]{1,0:T(8,128)S(1)}, f32[128,768]{1,0:T(8,128)}, u32[]{:S(2)}) copy-start(f32[128,768]{1,0:T(8,128)} %copy-done.34) | copy-start | bytes 1179652
  2038.4 35.8 %copy-start.39 = (bf16[1,128,768]{2,1,0:T(8,128)(2,1)S(1)}, bf16[1,128,768]{2,1,0:T(8,128)(2,1)}, u32[]{:S(2)}) copy-start(bf16[1,128,768]{2,1,0:T(8,128)(2,1)} %copy-done.38) | copy-start | bytes 589828
  2038.4 35.8 %copy-start.84 = (bf16[128,768]{1,0:T(8,128)(2,1)S(1)}, bf16[128,768]{1,0:T(8,128)(2,1)}, u32[]{:S(2)}) copy-start(bf16[128,768]{1,0:T(8,128)(2,1)} %all-reduce.52.cloned.1.call-done) | copy-start | bytes 589828
  2038.4 35.8 %copy-start.168 = (f32[128]{0:T(128)S(1)}, f32[128]{0:T(128)}, u32[]{:S(2)}) copy-start(f32[128]{0:T(128)} %copy-done.165) | copy-start | bytes 1540
  (434 other events, 2412.0 us)
Sparse Core Ops, SparseCore 0:
  216.8 28.4 all-reduce.37
  252.8 25.7 all-reduce.39
  485.7 25.7 all-reduce.41
  517.8 25.7 all-reduce.43
  751.5 25.8 all-reduce.45
  786.3 22.3 all-reduce.49
  1113.6 22.3 all-reduce.51
  1147.3 22.3 all-reduce.53
  1482.4 22.3 all-reduce.55
  1519.4 23.0 all-reduce.57
  1840.0 22.3 all-reduce.59
  1865.2 25.7 all-reduce.47
  2038.5 494.3 all-reduce.61
where the time goes:
time: 2630 us; the launch traced here: 2590 us
  waiting for transfers between devices  696 us (26%)
  other arithmetic  615 us (23%)
  matrix products  609 us (23%)
  local copies, waits for them, and re-layouts  580 us (22%)
  loops' own time  34.8 us (1%)
  blocking collectives  27.7 us (1%)
    dot_general x1008, matrix products, exact_dot(): return jnp.dot(left, right, precision=highest)  525 us
    psum x1, waiting for transfers between devices, shards(): totals = restore(lax.psum(flatten_all(totals), 'dp'), totals)  456 us
    squeeze x192, local copies, waits for them, and re-layouts, ttt_head(): lax.scan(jax.checkpoint(block_update), initial, (to_blocks(queries), to_b...  159 us
    concatenate x1, local copies, waits for them, and re-layouts, flatten_all(): return jnp.concatenate([jnp.ravel(part) for part in parts])  139 us
    add x96, other arithmetic, block_update(): flag * start + (1.0 - flag) * now  95.8 us
    psum x3, waiting for transfers between devices, forward(): lax.psum(jnp.dot(mixed_low, out_mat, preferred_element_type=jnp.float32),...  75.6 us
    dynamic_update_slice x72, other arithmetic, ttt_head(): lax.scan(jax.checkpoint(block_update), initial, (to_blocks(queries), to_b...  68.9 us
    dynamic_update_slice x96, local copies, waits for them, and re-layouts, ttt_head(): lax.scan(jax.checkpoint(block_update), initial, (to_blocks(queries), to_b...  66.1 us

commit v1 on v0

v1 whole, which is shorter than its diff:
```python
import functools
import jax
import jax.numpy as jnp
from jax import lax
from jax.experimental import pallas as pl
from jax.experimental.pallas import tpu as pltpu
from jax.sharding import PartitionSpec as P

MBT = 16
EPS = 1e-06
RATE = 0.125
C0 = 0.7978845608028654
BF = jnp.bfloat16
F32 = jnp.float32
VMEM = pl.BlockSpec(memory_space=pltpu.VMEM)
SMEM = pl.BlockSpec(memory_space=pltpu.SMEM)
ANY = pl.BlockSpec(memory_space=pl.ANY)
NRM, INV, MIS, MEANN, GZ2, NA, INVA, NO, INVO, GATE = range(10)
INNER_ROWS = 832


def dot(a, b):
    return jnp.dot(a, b, preferred_element_type=F32)


def dot_t(a, b):
    return lax.dot_general(a, b, (((1,), (1,)), ((), ())), preferred_element_type=F32)


def tdot(a, b):
    return lax.dot_general(a, b, (((0,), (0,)), ((), ())), preferred_element_type=F32)


def cat(parts, axis):
    return jnp.concatenate(parts, axis=axis)


def gelu_parts(z):
    z2 = z * z
    t = jnp.tanh(C0 * z * (1.0 + 0.044715 * z2))
    h = 0.5 * (1.0 + t)
    du = C0 * (1.0 + 0.134145 * z2)
    sech = 1.0 - t * t
    value = z * h
    slope = h + 0.5 * z * sech * du
    return value, slope, t, z2, du, sech


def gelu_two(z):
    value, slope, _, _, _, _ = gelu_parts(z)
    return value, slope


def gelu_curve(z):
    _, _, t, z2, du, sech = gelu_parts(z)
    return sech * (C0 * (1.0 + 0.26829 * z2) - z * t * du * du)


def rms_inv(values):
    return lax.rsqrt(jnp.mean(values * values, axis=-1, keepdims=True) + EPS)


class Pick:
    def __init__(self, layer, sems):
        self.own = lax.axis_index("segment") == layer
        self.sems = sems
        self.count = 0

    def start(self, own_ref, other_ref, dst):
        sem = self.sems.at[self.count]
        self.count += 1

        @pl.when(self.own)
        def _():
            pltpu.make_async_copy(own_ref, dst, sem).start()

        @pl.when(jnp.logical_not(self.own))
        def _():
            pltpu.make_async_copy(other_ref, dst, sem).start()

        return pltpu.make_async_copy(own_ref, dst, sem)


def doc_places(dl_ref, steps):
    core = lax.axis_index("segment")
    one, two = dl_ref[core, 0], dl_ref[core, 1]
    begin = jnp.where(one == steps, 0, jnp.where(two == steps, one, one + two))
    cut = jnp.where(one == steps, two, one)
    return begin, cut


def block_starts(begin, steps):
    places = []
    for s in range(steps):
        places.append(pl.multiple_of((begin + s) * MBT, MBT))
        places.append(pl.multiple_of(jnp.where(s < begin, s, s + steps) * MBT, MBT))
    return places


def gather_rows(ref, lead, places):
    return cat([ref[lead, pl.ds(p, MBT), :] for p in places], 0)


def scatter_rows(ref, places, value):
    for i, p in enumerate(places):
        ref[pl.ds(p, MBT), :] = value[i * MBT : (i + 1) * MBT, :]


def masks(cut, length):
    def parts(axis):
        i = lax.broadcasted_iota(jnp.int32, (length, length), axis)
        step, lane, t = i >> 5, (i >> 4) & 1, i & 15
        doc = jnp.where(lane == 0, 0, jnp.where(step < cut, 1, 2))
        return step, lane, t, doc

    s0, l0, t0, d0 = parts(0)
    s1, l1, t1, d1 = parts(1)
    same = d0 == d1
    block = (s0 == s1) & (l0 == l1)
    past = jnp.where(same & (s1 < s0), 1.0 / MBT, 0.0)
    past_t = jnp.where(same & (s0 < s1), 1.0 / MBT, 0.0)
    inside = jnp.where(block & (t1 <= t0), 1.0 / (t0 + 1).astype(F32), 0.0)
    inside_t = jnp.where(block & (t0 <= t1), 1.0 / (t1 + 1).astype(F32), 0.0)
    return past, past + inside, past_t, past_t + inside_t


class Halves:
    def __init__(self):
        lane = lax.broadcasted_iota(jnp.int32, (1, 128), 1)
        self.left = lane < 64
        r = lax.broadcasted_iota(jnp.int32, (256, 128), 0) & 127
        c = lax.broadcasted_iota(jnp.int32, (256, 128), 1)
        self.mean_mat = jnp.where((r < 64) == (c < 64), 1.0 / 64.0, 0.0).astype(BF)

    def mean(self, x):
        high = x.astype(BF)
        low = (x - high.astype(F32)).astype(BF)
        return dot(cat([high, low], 1), self.mean_mat)

    def split(self, x):
        zero = jnp.zeros_like(x)
        return cat([jnp.where(self.left, x, zero), jnp.where(self.left, zero, x)], 0)

    def pack(self, a, b):
        return jnp.where(self.left, a, b)


def pair_weights(inner_ref, small_ref, heads, p, halves):
    width = inner_ref.shape[2]
    zero = jnp.zeros((64, width), BF)

    def blocks(a, b):
        return cat([cat([a, zero], 1), cat([zero, b], 1)], 0)

    def centred(index):
        w = inner_ref[heads + index].astype(F32)
        return (w - jnp.mean(w, axis=0, keepdims=True)).astype(BF)

    w1 = blocks(inner_ref[2 * p], inner_ref[2 * p + 1])
    w2 = blocks(centred(2 * p), centred(2 * p + 1))
    return w1, w2


def pad_rows(parts, rows):
    have = sum(x.shape[0] for x in parts)
    if have < rows:
        parts = parts + [jnp.zeros((rows - have, parts[0].shape[1]), parts[0].dtype)]
    return cat(parts, 0) if len(parts) > 1 else parts[0]


def mixer_forward(refs, x_one, mix_ref, rate_ref, inner_ref, small_ref, begin_cut, x1_ready):
    (mixed_ref, stats_ref, kq_ref, x2_ref, g1_ref, y2_ref, d1_ref, ud2_ref, e1_ref, sm_ref, sg_ref) = refs
    _, cut = begin_cut
    length = x_one.shape[0]
    heads = inner_ref.shape[0] // 2
    pairs = heads // 2
    hid = inner_ref.shape[2]
    wide = heads * 64
    steps = length // (2 * MBT)
    rows = 2 * MBT
    past, near, _, _ = masks(cut, length)
    hv = Halves()
    proj = dot(x_one, mix_ref[...])
    logits = dot_t(x_one, rate_ref[...]) + small_ref[3:4, 0:16]
    sg = jax.nn.sigmoid(logits)
    sg_ref[...] = sg
    stats_ref[...] = cat(
        [jnp.mean(sg, axis=0, keepdims=True), jnp.max(sg, axis=0, keepdims=True)], 0
    )
    rates = RATE * sg
    st = []
    for p in range(pairs):
        c = slice(128 * p, 128 * p + 128)
        h = slice(2 * hid * p, 2 * hid * (p + 1))
        q, k, v, gate = [proj[:, wide * i + 128 * p : wide * i + 128 * p + 128] for i in range(4)]
        d = dict(q=q, gate=gate, diff=v - k, c=c, h=h)
        d["w1"], d["w2"] = pair_weights(inner_ref, small_ref, heads, p, hv)
        d["b1"] = small_ref[0:1, h]
        b2 = small_ref[2:3, 128 * p : 128 * p + 128]
        d["b2"] = b2 - hv.mean(jnp.broadcast_to(b2, (8, 128)))[0:1]
        d["g"] = small_ref[2:3, wide + 128 * p : wide + 128 * p + 128]
        d["gp"] = small_ref[2:3, 2 * wide + 128 * p : 2 * wide + 128 * p + 128]
        d["be"] = small_ref[2:3, 3 * wide + 128 * p : 3 * wide + 128 * p + 128]
        d["r"] = [rates[:, 2 * p + i : 2 * p + i + 1] for i in range(2)]
        d["rp"] = hv.pack(d["r"][0], d["r"][1])
        d["kb"], d["qb"] = k.astype(BF), q.astype(BF)
        kq_ref[:, c] = d["kb"]
        kq_ref[:, wide + 128 * p : wide + 128 * p + 128] = d["qb"]
        d["base"] = dot(d["kb"], d["w1"]) + d["b1"]
        kk = dot_t(hv.split(d["kb"]), d["kb"])
        d["m1"] = [(past * (kk[i * length : (i + 1) * length] + 1.0)).astype(BF) for i in range(2)]
        for name in ("x2", "g1", "g2", "z1", "u"):
            d[name] = []
        st.append(d)
    for s in range(steps):
        sl = slice(rows * s, rows * s + rows)
        for p in range(pairs):
            d = st[p]
            c, h = d["c"], d["h"]
            z1 = d["base"][sl]
            if s:
                g1 = pad_rows(d["g1"], length)
                x2 = pad_rows(d["x2"], length)
                g2 = pad_rows(d["g2"], length)
                z1 = z1 - cat([dot(d["m1"][i][sl], g1[:, hid * i : hid * (i + 1)]) for i in range(2)], 1)
            act, slope = gelu_two(z1)
            actb = act.astype(BF)
            z2 = dot_t(actb, d["w2"]) + d["b2"]
            if s:
                far = [
                    (past[sl] * (dot_t(actb[:, hid * i : hid * (i + 1)], x2[:, hid * i : hid * (i + 1)]) + 1.0)).astype(BF)
                    for i in range(2)
                ]
                z2 = z2 - dot(cat(far, 1), hv.split(g2))
            inv = lax.rsqrt(hv.mean(z2 * z2) + EPS)
            n = z2 * inv
            mis = n * d["g"] + d["be"] - d["diff"][sl]
            misg = mis * d["g"]
            both = hv.mean(cat([misg, misg * n], 0))
            gz2 = (misg - both[:rows] - n * both[rows:]) * inv
            gz2b = gz2.astype(BF)
            u = dot(gz2b, d["w2"])
            if s:
                f = dot_t(hv.split(gz2b), g2)
                u = u - cat(
                    [
                        dot((past[sl] * f[rows * i : rows * (i + 1)]).astype(BF), x2[:, hid * i : hid * (i + 1)])
                        for i in range(2)
                    ],
                    1,
                )
            gz1 = u * slope
            r0, r1 = d["r"][0][sl], d["r"][1][sl]
            g1n = cat([gz1[:, :hid] * r0, gz1[:, hid:] * r1], 1).astype(BF)
            g2n = (gz2 * d["rp"][sl]).astype(BF)
            d["x2"].append(actb)
            d["g1"].append(g1n)
            d["g2"].append(g2n)
            d["z1"].append(z1)
            d["u"].append(u)
            x2_ref[sl, h] = actb
            g1_ref[sl, h] = g1n
            d1_ref[sl, h] = slope.astype(BF)
            sm_ref[NRM, sl, c] = n
            sm_ref[INV, sl, c] = inv
            sm_ref[MIS, sl, c] = mis
            sm_ref[MEANN, sl, c] = both[rows:]
            sm_ref[GZ2, sl, c] = gz2
    mixed = []
    for p in range(pairs):
        d = st[p]
        c, h = d["c"], d["h"]
        g1, x2, g2 = cat(d["g1"], 0), cat(d["x2"], 0), cat(d["g2"], 0)
        ud2_ref[:, h] = (cat(d["u"], 0) * gelu_curve(cat(d["z1"], 0))).astype(BF)
        qk = dot_t(hv.split(d["qb"]), d["kb"])
        corr = [
            dot((near * (qk[length * i : length * (i + 1)] + 1.0)).astype(BF), g1[:, hid * i : hid * (i + 1)])
            for i in range(2)
        ]
        act, slope = gelu_two(dot(d["qb"], d["w1"]) + d["b1"] - cat(corr, 1))
        actb = act.astype(BF)
        y2_ref[:, h] = actb
        e1_ref[:, h] = slope.astype(BF)
        far = [
            (near * (dot_t(actb[:, hid * i : hid * (i + 1)], x2[:, hid * i : hid * (i + 1)]) + 1.0)).astype(BF)
            for i in range(2)
        ]
        a2 = dot_t(actb, d["w2"]) + d["b2"] - dot(cat(far, 1), hv.split(g2))
        inv_a = lax.rsqrt(hv.mean(a2 * a2) + EPS)
        n_a = a2 * inv_a
        out = d["q"] + n_a * d["g"] + d["be"]
        inv_o = lax.rsqrt(hv.mean(out * out) + EPS)
        n_o = out * inv_o
        gated, _ = gelu_two(d["gate"])
        low = (gated * n_o * d["gp"]).astype(BF)
        mixed_ref[:, c] = low
        mixed.append(low)
        sm_ref[NA, :, c] = n_a
        sm_ref[INVA, :, c] = inv_a
        sm_ref[NO, :, c] = n_o
        sm_ref[INVO, :, c] = inv_o
        sm_ref[GATE, :, c] = d["gate"]
    return cat(mixed, 1)


def mixer_backward(dmixed, mixed_refs, inner_ref, small_ref, begin_cut, ig_ref):
    (kq_ref, x2_ref, g1_ref, y2_ref, d1_ref, ud2_ref, e1_ref, sm_ref, sg_ref) = mixed_refs
    _, cut = begin_cut
    length = dmixed.shape[0]
    heads = inner_ref.shape[0] // 2
    pairs = heads // 2
    hid = inner_ref.shape[2]
    wide = heads * 64
    steps = length // (2 * MBT)
    rows = 2 * MBT
    past, near, past_t, near_t = masks(cut, length)
    hv = Halves()
    sg = sg_ref[...]
    rates = RATE * sg

    def by_head(fn):
        return [fn(slice(hid * i, hid * (i + 1)), i) for i in range(2)]

    st = []
    for p in range(pairs):
        c = slice(128 * p, 128 * p + 128)
        h = slice(2 * hid * p, 2 * hid * (p + 1))
        d = dict(c=c, h=h)
        d["w1"], d["w2"] = pair_weights(inner_ref, small_ref, heads, p, hv)
        g = small_ref[2:3, wide + 128 * p : wide + 128 * p + 128]
        gp = small_ref[2:3, 2 * wide + 128 * p : 2 * wide + 128 * p + 128]
        d["g"] = g
        d["r"] = [rates[:, 2 * p + i : 2 * p + i + 1] for i in range(2)]
        d["rp"] = hv.pack(d["r"][0], d["r"][1])
        kb = kq_ref[:, c]
        qb = kq_ref[:, wide + 128 * p : wide + 128 * p + 128]
        x2, g1, y2 = x2_ref[:, h], g1_ref[:, h], y2_ref[:, h]
        gz2 = sm_ref[GZ2, :, c]
        gz2b = gz2.astype(BF)
        g2b = (gz2 * d["rp"]).astype(BF)
        dm = dmixed[:, c]
        gate = sm_ref[GATE, :, c]
        n_o, inv_o = sm_ref[NO, :, c], sm_ref[INVO, :, c]
        n_a, inv_a = sm_ref[NA, :, c], sm_ref[INVA, :, c]
        gated, gate_slope = gelu_two(gate)
        d["dgate"] = dm * n_o * gp * gate_slope
        drm = dm * gated
        d["dgp"] = jnp.sum(drm * n_o, axis=0, keepdims=True)
        dpg = drm * gp
        do = (dpg - n_o * hv.mean(dpg * n_o)) * inv_o
        dn = do * g
        both = hv.mean(cat([dn, dn * n_a], 0))
        da2 = (dn - both[:length] - n_a * both[length:]) * inv_a
        d["dg"] = jnp.sum(do * n_a, axis=0, keepdims=True)
        d["dbe"] = jnp.sum(do, axis=0, keepdims=True)
        d["db2"] = jnp.sum(da2, axis=0, keepdims=True)
        da2b = da2.astype(BF)
        da2m, g2m = hv.split(da2b), hv.split(g2b)
        km, qm = hv.split(kb), hv.split(qb)

        def weigh(mask, full, i):
            return (mask * full[length * i : length * (i + 1)]).astype(BF)

        p2 = dot_t(da2m, g2b)
        p2t = dot_t(g2m, da2b)
        dy2 = dot(da2b, d["w2"]) - cat(by_head(lambda e, i: dot(weigh(near, p2, i), x2[:, e])), 1)
        d["bx2"] = cat(by_head(lambda e, i: dot(weigh(near_t, p2t, i), y2[:, e])), 1)
        syt = cat(by_head(lambda e, i: (near_t * (dot_t(x2[:, e], y2[:, e]) + 1.0)).astype(BF)), 1)
        d["bg2"] = -dot(syt, da2m)
        da1 = dy2 * e1_ref[:, h].astype(F32)
        da1b = da1.astype(BF)
        d["db1"] = jnp.sum(da1, axis=0, keepdims=True)
        p1 = cat(by_head(lambda e, i: (near * dot_t(da1b[:, e], g1[:, e])).astype(BF)), 1)
        p1t = cat(by_head(lambda e, i: (near_t * dot_t(g1[:, e], da1b[:, e])).astype(BF)), 1)
        d["dq"] = do + dot_t(da1b, d["w1"]) - dot(p1, km)
        d["dk"] = -dot(p1t, qm)
        kq = dot_t(km, qb) + 1.0
        kk = dot_t(km, kb) + 1.0
        d["bg1"] = cat(by_head(lambda e, i: dot(weigh(near_t, kq, i), da1b[:, e])), 1)
        d["m1t"] = [weigh(past_t, kk, i) for i in range(2)]
        d["rx"] = by_head(lambda e, i: (past_t * (dot_t(x2[:, e], x2[:, e]) + 1.0)).astype(BF))
        ft = dot_t(g2m, gz2b)
        d["ft"] = [weigh(past_t, ft, i) for i in range(2)]
        d.update(x2=x2, y2=y2, g1=g1, g2b=g2b, g2m=g2m, gz2=gz2, gz2b=gz2b, gz2m=hv.split(gz2b))
        d.update(km=km, kb=kb, qb=qb, da1b=da1b, da2b=da2b)
        for name in ("z1", "z2", "u", "rg1", "rg2", "t"):
            d[name] = [None] * steps
        st.append(d)
    for s in reversed(range(steps)):
        sl = slice(rows * s, rows * s + rows)
        later = rows * (s + 1)
        for p in range(pairs):
            d = st[p]
            c, h = d["c"], d["h"]
            x2 = d["x2"]
            bg1, bg2, bx2 = -d["bg1"][sl], d["bg2"][sl], -d["bx2"][sl]
            if s < steps - 1:

                def full(parts):
                    done = parts[s + 1 :]
                    return cat([jnp.zeros((later, done[0].shape[1]), BF)] + done, 0)

                z1l, z2l, ul = full(d["z1"]), full(d["z2"]), full(d["u"])
                bg1 = bg1 - cat(by_head(lambda e, i: dot(d["m1t"][i][sl], z1l[:, e])), 1)
                xu = by_head(lambda e, i: (past_t[sl] * dot_t(x2[sl, e], ul[:, e])).astype(BF))
                lhs = cat([d["rx"][0][sl], d["rx"][1][sl]] + xu, 1)
                bg2 = bg2 - dot(lhs, cat([hv.split(z2l), d["gz2m"]], 0))
                gz = dot_t(hv.split(d["g2b"][sl]), z2l)
                bx2 = bx2 - cat(
                    by_head(
                        lambda e, i: dot(
                            cat([(past_t[sl] * gz[rows * i : rows * (i + 1)]).astype(BF), d["ft"][i][sl]], 1),
                            cat([x2[:, e], ul[:, e]], 0),
                        )
                    ),
                    1,
                )
            r0, r1 = d["r"][0][sl], d["r"][1][sl]
            dgz1 = cat([bg1[:, :hid] * r0, bg1[:, hid:] * r1], 1)
            slope = d1_ref[sl, h].astype(F32)
            du = dgz1 * slope
            dub = du.astype(BF)
            dz1 = dgz1 * ud2_ref[sl, h].astype(F32)
            dgz2 = bg2 * d["rp"][sl] + dot_t(dub, d["w2"])
            if s:
                hm = by_head(lambda e, i: (past[sl] * dot_t(dub[:, e], x2[:, e])).astype(BF))
                dgz2 = dgz2 - dot(cat(hm, 1), d["g2m"])
            n, inv = sm_ref[NRM, sl, c], sm_ref[INV, sl, c]
            mis, mn = sm_ref[MIS, sl, c], sm_ref[MEANN, sl, c]
            g = d["g"]
            e = dgz2 * inv
            three = hv.mean(cat([e, e * n, dgz2 * d["gz2"][sl]], 0))
            dmis = e - three[:rows] - n * three[rows : 2 * rows]
            t = dmis * g
            dn = t * g - e * mn - mis * g * three[rows : 2 * rows]
            two = hv.mean(cat([dn, dn * n], 0))
            dz2 = inv * (dn - two[:rows] - n * (two[rows:] + three[2 * rows :]))
            d["dg"] = d["dg"] + jnp.sum(t * n + dmis * mis, axis=0, keepdims=True)
            d["dbe"] = d["dbe"] + jnp.sum(t, axis=0, keepdims=True)
            d["db2"] = d["db2"] + jnp.sum(dz2, axis=0, keepdims=True)
            dz2b = dz2.astype(BF)
            dx2 = bx2 + dot(dz2b, d["w2"])
            if s:
                j = dot_t(hv.split(dz2b), d["g2b"])
                dx2 = dx2 - cat(
                    by_head(lambda e, i: dot((past[sl] * j[rows * i : rows * (i + 1)]).astype(BF), x2[:, e])), 1
                )
            dz1 = dz1 + dx2 * slope
            d["db1"] = d["db1"] + jnp.sum(dz1, axis=0, keepdims=True)
            d["z1"][s], d["z2"][s], d["u"][s] = dz1.astype(BF), dz2b, dub
            d["rg1"][s], d["rg2"][s], d["t"][s] = bg1, bg2, t
    parts = [[], [], [], []]
    rate_cols = []
    for p in range(pairs):
        d = st[p]
        z1, z2, u = cat(d["z1"], 0), cat(d["z2"], 0), cat(d["u"], 0)
        t = cat(d["t"], 0)
        g1 = d["g1"]
        both = cat(
            by_head(
                lambda e, i: (past * dot_t(z1[:, e], g1[:, e]) + past_t * dot_t(g1[:, e], z1[:, e])).astype(BF)
            ),
            1,
        )
        dk = d["dk"] + t + dot_t(z1, d["w1"]) - dot(both, d["km"])
        for i, value in enumerate((d["dq"], dk, -t, d["dgate"])):
            parts[i].append(value.astype(BF))
        dw1 = tdot(cat([d["kb"], d["qb"]], 0), cat([z1, d["da1b"]], 0))
        dw2 = tdot(cat([z2, d["da2b"], d["gz2b"]], 0), cat([d["x2"], d["y2"], u], 0))
        for i in range(2):
            row = 64 * (2 * p + i)
            ig_ref[row : row + 64, :] = dw1[64 * i : 64 * i + 64, hid * i : hid * (i + 1)]
            row = row + 64 * heads
            ig_ref[row : row + 64, :] = dw2[64 * i : 64 * i + 64, hid * i : hid * (i + 1)]
            ig_ref[786 + 2 * p + i : 787 + 2 * p + i, :] = d["db1"][:, hid * i : hid * (i + 1)]
        one = cat(d["rg1"], 0) * g1.astype(F32)
        two = cat(d["rg2"], 0) * d["g2b"].astype(F32)
        two = cat([jnp.where(hv.left, two, 0.0), jnp.where(hv.left, 0.0, two)], 1)
        for i in range(2):
            whole = one[:, hid * i : hid * i + 128] + one[:, hid * i + 128 : hid * (i + 1)]
            whole = whole + two[:, 128 * i : 128 * (i + 1)]
            rate_cols.append(jnp.sum(whole, axis=-1, keepdims=True))
        for j, name in enumerate(("db2", "dg", "dgp", "dbe")):
            piece = 3 * j + p
            ig_ref[792 + piece // 2 : 793 + piece // 2, 128 * (piece % 2) : 128 * (piece % 2) + 128] = d[name]
    lane = lax.broadcasted_iota(jnp.int32, (1, 16), 1)
    dlog = jnp.zeros((length, 16), F32)
    for i, col in enumerate(rate_cols):
        dlog = dlog + jnp.where(lane == i, col, 0.0)
    dlog = dlog * (1.0 - sg)
    ig_ref[798:799, 0:16] = jnp.sum(dlog, axis=0, keepdims=True)
    dmix = [cat(x, 1) for x in parts]
    return dmix, dlog.astype(BF)


def ka_body(layer, *args):
    if layer == 0:
        dl_ref, li_ref = args[:2]
        rest = args[2:]
    else:
        dl_ref, h1_ref, fo_ref, fr_ref = args[:4]
        rest = args[4:]
    wrefs, rest = rest[:10], rest[10:]
    if layer == 1:
        lo_ref, rest = rest[0], rest[1:]
    hb_ref, x1_ref, att_ref = rest[:3]
    saves, scratch = rest[3:14], rest[14:]
    mix_v, inner_v, small_v, rate_v, out_v, sems = scratch
    pick = Pick(layer, sems)
    c_small = pick.start(wrefs[0], wrefs[1], small_v)
    c_mix = pick.start(wrefs[2], wrefs[3], mix_v)
    c_rate = pick.start(wrefs[4], wrefs[5], rate_v)
    c_inner = pick.start(wrefs[6], wrefs[7], inner_v)
    c_out = pick.start(wrefs[8], wrefs[9], out_v)
    length = hb_ref.shape[0]
    steps = length // (2 * MBT)
    begin, cut = doc_places(dl_ref, steps)
    places = block_starts(begin, steps)
    if layer == 0:
        low = gather_rows(li_ref, lax.axis_index("segment"), places)
    else:
        low = (h1_ref[...] + (fo_ref[...].astype(F32) + fr_ref[...].astype(F32))).astype(BF)
        scatter_rows(lo_ref, places, low)
    hb_ref[...] = low
    h = low.astype(F32)
    inv = rms_inv(h)
    c_small.wait()
    x_one = (h * inv * small_v[1:2, 0 : h.shape[1]]).astype(BF)
    x1_ref[...] = x_one
    c_mix.wait()
    c_rate.wait()
    c_inner.wait()
    mixed = mixer_forward(saves, x_one, mix_v, rate_v, inner_v, small_v, (begin, cut), None)
    c_out.wait()
    att_ref[...] = dot(mixed, out_v[...]).astype(BF)


def ffn_forward(h1, small_v, sw_v, dn_v, copies):
    width = h1.shape[1]
    inv = rms_inv(h1)
    x2 = (h1 * inv * small_v[1:2, width : 2 * width]).astype(BF)
    copies[0].wait()
    up_at = sw_v.shape[1] // 2
    gate = dot(x2, sw_v[:, :up_at])
    up = dot(x2, sw_v[:, up_at:])
    sgm = 1.0 / (1.0 + jnp.exp(-gate))
    silu = gate * sgm
    slope = up * (sgm * (1.0 + gate * (1.0 - sgm)))
    hidden = (silu * up).astype(BF)
    copies[1].wait()
    feed = dot(hidden, dn_v[...]).astype(BF)
    return x2, hidden, slope, silu, feed


def ffn_backward(dfe, slope, silu, sw_v, dn_v):
    up_at = sw_v.shape[1] // 2
    dh = dot_t(dfe, dn_v[...])
    dg, du = (dh * slope).astype(BF), (dh * silu).astype(BF)
    dx = dot_t(dg, sw_v[:, :up_at]) + dot_t(du, sw_v[:, up_at:])
    return dg, du, dx.astype(BF)


def pack_ffn(keep_ref, send_ref, x2, dg, du, hidden, dfe):
    first = lax.axis_index("segment") == 0
    width, wide = x2.shape[1], dg.shape[1]
    half = wide // 2

    def put(ref, grad, hid):
        ref[:, 0:width] = x2
        ref[:, width : width + wide] = grad
        ref[:, width + wide : width + wide + half] = hid
        ref[:, width + wide + half :] = dfe

    @pl.when(first)
    def _():
        put(keep_ref, dg, hidden[:, :half])
        put(send_ref, du, hidden[:, half:])

    @pl.when(jnp.logical_not(first))
    def _():
        put(keep_ref, du, hidden[:, half:])
        put(send_ref, dg, hidden[:, :half])


def kf_body(hb_ref, ao_ref, ar_ref, s_own, s_oth, w_own, w_oth, d_own, d_oth,
            h1_ref, x2_ref, hid_ref, sl_ref, si_ref, fe_ref, small_v, sw_v, dn_v, sems):
    pick = Pick(0, sems)
    c_small = pick.start(s_own, s_oth, small_v)
    copies = [pick.start(w_own, w_oth, sw_v), pick.start(d_own, d_oth, dn_v)]
    h1 = hb_ref[...].astype(F32) + (ao_ref[...].astype(F32) + ar_ref[...].astype(F32))
    h1_ref[...] = h1
    c_small.wait()
    x2, hidden, slope, silu, feed = ffn_forward(h1, small_v, sw_v, dn_v, copies)
    x2_ref[...] = x2
    hid_ref[...] = hidden
    sl_ref[...] = slope.astype(BF)
    si_ref[...] = silu.astype(BF)
    fe_ref[...] = feed


def kfb_body(dl_ref, ct_ref, hb_ref, ao_ref, ar_ref, s_own, s_oth, w_own, w_oth, d_own, d_oth,
             h1_ref, fe_ref, dxt_ref, dfe_ref, keep_ref, send_ref, small_v, sw_v, dn_v, sems):
    pick = Pick(1, sems)
    c_small = pick.start(s_own, s_oth, small_v)
    copies = [pick.start(w_own, w_oth, sw_v), pick.start(d_own, d_oth, dn_v)]
    length = hb_ref.shape[0]
    steps = length // (2 * MBT)
    begin, _ = doc_places(dl_ref, steps)
    dfe = gather_rows(ct_ref, lax.axis_index("segment"), block_starts(begin, steps))
    dfe_ref[...] = dfe
    h1 = hb_ref[...].astype(F32) + (ao_ref[...].astype(F32) + ar_ref[...].astype(F32))
    h1_ref[...] = h1
    c_small.wait()
    x2, hidden, slope, silu, feed = ffn_forward(h1, small_v, sw_v, dn_v, copies)
    fe_ref[...] = feed
    dg, du, dx = ffn_backward(dfe, slope, silu, sw_v, dn_v)
    dxt_ref[...] = dx
    pack_ffn(keep_ref, send_ref, x2, dg, du, hidden, dfe)


def norm_back(dx, x, gain, base):
    inv = rms_inv(x)
    e = dx * gain
    grad = base + e * inv - x * (jnp.mean(e * x, axis=-1, keepdims=True) * inv * inv * inv)
    gain_grad = jnp.sum(dx * x * inv, axis=0, keepdims=True)
    return grad, gain_grad


def kbf_body(dl_ref, hb_ref, dh_ref, xo_ref, xr_ref, t_own, t_oth, x2_ref, hid_ref, sl_ref, si_ref,
             w_own, w_oth, d_own, d_oth,
             ig_ref, gg_ref, dfe_ref, dxt_ref, keep_ref, send_ref, small_v, sw_v, dn_v, sems, sems_two):
    above = Pick(1, sems)
    c_small = above.start(t_own, t_oth, small_v)
    pick = Pick(0, sems_two)
    copies = [pick.start(d_own, d_oth, dn_v), pick.start(w_own, w_oth, sw_v)]
    length, width = hb_ref.shape
    steps = length // (2 * MBT)
    begin, _ = doc_places(dl_ref, steps)
    dx = xo_ref[...].astype(F32) + xr_ref[...].astype(F32)
    c_small.wait()
    grad, gain = norm_back(dx, hb_ref[...].astype(F32), small_v[1:2, 0:width], dh_ref[...])
    scatter_rows(ig_ref, block_starts(begin, steps), grad)
    gg_ref[...] = gain
    dfe = grad.astype(BF)
    dfe_ref[...] = dfe
    for c in copies:
        c.wait()
    dg, du, dxt = ffn_backward(dfe, sl_ref[...].astype(F32), si_ref[...].astype(F32), sw_v, dn_v)
    dxt_ref[...] = dxt
    pack_ffn(keep_ref, send_ref, x2_ref[...], dg, du, hid_ref[...], dfe)


def kba_body(layer, dl_ref, xo_ref, xr_ref, dy_ref, h1_ref, x1_ref, mixed_ref, *rest):
    saves, rest = rest[:9], rest[9:]
    wrefs, rest = rest[:10], rest[10:]
    dh_ref, dxo_ref, keep_ref, send_ref, ig_ref, mix_v, inner_v, small_v, rate_v, out_v, sems = rest
    pick = Pick(layer, sems)
    c_small = pick.start(wrefs[0], wrefs[1], small_v)
    c_out = pick.start(wrefs[8], wrefs[9], out_v)
    c_inner = pick.start(wrefs[6], wrefs[7], inner_v)
    c_mix = pick.start(wrefs[2], wrefs[3], mix_v)
    c_rate = pick.start(wrefs[4], wrefs[5], rate_v)
    length, width = h1_ref.shape
    steps = length // (2 * MBT)
    place = doc_places(dl_ref, steps)
    dx = xo_ref[...].astype(F32) + xr_ref[...].astype(F32)
    c_small.wait()
    dh, gain = norm_back(dx, h1_ref[...], small_v[1:2, width : 2 * width], dy_ref[...].astype(F32))
    dh_ref[...] = dh
    ig_ref[768:INNER_ROWS, :] = jnp.zeros((INNER_ROWS - 768, ig_ref.shape[1]), F32)
    for j in range(3):
        ig_ref[799 + j : 800 + j, :] = gain[:, 256 * j : 256 * j + 256]
    da = dh.astype(BF)
    c_out.wait()
    c_inner.wait()
    dmixed = dot_t(da, out_v[...])
    dmix, dlog = mixer_backward(dmixed, saves, inner_v, small_v, place, ig_ref)
    x1 = x1_ref[...]
    drate = tdot(dlog, x1)
    heads = inner_v.shape[0] // 2
    for j in range(3):
        ig_ref[768 + heads * j : 768 + heads * (j + 1), :] = drate[:heads, 256 * j : 256 * j + 256]
    c_mix.wait()
    c_rate.wait()
    dxo_ref[...] = (dot_t(cat(dmix, 1), mix_v[...]) + dot(dlog, rate_v[...])).astype(BF)
    first = lax.axis_index("segment") == 0
    half = width // 2
    wide = 2 * dmix[0].shape[1]

    def put(ref, one, two, att):
        ref[:, 0:width] = x1
        ref[:, width : width + wide // 2] = one
        ref[:, width + wide // 2 : width + wide] = two
        ref[:, width + wide : width + wide + mixed_ref.shape[1]] = mixed_ref[...]
        ref[:, width + wide + mixed_ref.shape[1] :] = att

    @pl.when(first)
    def _():
        put(keep_ref, dmix[0], dmix[1], da[:, :half])
        put(send_ref, dmix[2], dmix[3], da[:, half:])

    @pl.when(jnp.logical_not(first))
    def _():
        put(keep_ref, dmix[2], dmix[3], da[:, half:])
        put(send_ref, dmix[0], dmix[1], da[:, :half])


def ke_body(dl_ref, hb_ref, dh_ref, xo_ref, xr_ref, s_own, s_oth, ig_ref, gg_ref, small_v, sems):
    pick = Pick(0, sems)
    c_small = pick.start(s_own, s_oth, small_v)
    length, width = hb_ref.shape
    steps = length // (2 * MBT)
    begin, _ = doc_places(dl_ref, steps)
    dx = xo_ref[...].astype(F32) + xr_ref[...].astype(F32)
    c_small.wait()
    grad, gain = norm_back(dx, hb_ref[...].astype(F32), small_v[1:2, 0:width], dh_ref[...])
    scatter_rows(ig_ref, block_starts(begin, steps), grad)
    gg_ref[...] = gain


def kgf_body(keep_ref, recv_ref, dsw_ref, ddn_ref):
    both = cat([keep_ref[...], recv_ref[...]], 0)
    width, wide, half = dsw_ref.shape[0], dsw_ref.shape[1], ddn_ref.shape[0]
    dsw_ref[...] = tdot(both[:, :width], both[:, width : width + wide]).astype(BF)
    ddn_ref[...] = tdot(both[:, width + wide : width + wide + half], both[:, width + wide + half :]).astype(BF)


def kga_body(keep_ref, recv_ref, ik_ref, ir_ref, dmx_ref, dow_ref, din_ref):
    both = cat([keep_ref[...], recv_ref[...]], 0)
    width, wide, heads_wide = dmx_ref.shape[0], dmx_ref.shape[1], dow_ref.shape[0]
    dmx_ref[...] = tdot(both[:, :width], both[:, width : width + wide]).astype(BF)
    dow_ref[...] = tdot(both[:, width + wide : width + wide + heads_wide], both[:, width + wide + heads_wide :]).astype(BF)
    rows = din_ref.shape[0]
    at = pl.multiple_of(lax.axis_index("segment") * rows, rows)
    din_ref[...] = (ik_ref[pl.ds(at, rows), :] + ir_ref[pl.ds(at, rows), :]).astype(BF)


def call(body, name, ins, specs, outs, scratch=(), flops=2e8, nbytes=8e6):
    return pl.pallas_call(
        body,
        out_shape=[jax.ShapeDtypeStruct(s, t) for s, t in outs],
        in_specs=specs,
        out_specs=[VMEM] * len(outs),
        scratch_shapes=list(scratch),
        compiler_params=pltpu.CompilerParams(vmem_limit_bytes=48 * 1024 * 1024),
        cost_estimate=pl.CostEstimate(flops=int(flops), bytes_accessed=int(nbytes), transcendentals=0),
        name=name,
    )(*ins)


def swap(value, axis):
    return lax.ppermute(value, axis, [(0, 1), (1, 0)])


def shards(
    layer_input, doc_lengths, norm_gains, mixing, rate_weight, rate_offset, expand, hidden_bias, contract,
    result_bias, head_gains, head_shift, output_proj, swiglu, down_proj, cotangent,
):
    micro, _, length, width = layer_input.shape
    heads = rate_weight.shape[2]
    hid = expand.shape[3]
    wide = heads * 64
    ff = down_proj.shape[1]
    first = lax.axis_index("segment") == 0
    dl = doc_lengths.reshape(micro, 3)
    li = layer_input.reshape(micro, length, width)
    ct = cotangent.reshape(micro, length, width)
    small = jnp.stack(
        [
            hidden_bias.reshape(-1),
            norm_gains.reshape(-1),
            cat([result_bias.reshape(-1), head_gains.reshape(-1), head_shift.reshape(-1)], 0),
            jnp.pad(rate_offset.reshape(-1), (0, heads * hid - heads)),
        ]
    )
    mix = mixing[0].reshape(width, -1)
    rate = jnp.pad(rate_weight[0].T, ((0, 16 - heads), (0, 0)))
    inner = cat([expand[0], jnp.swapaxes(contract[0], 1, 2)], 0).astype(BF)
    ow = output_proj[0]
    sw = swiglu[0].reshape(width, -1)
    dn = down_proj[0]

    def both(x):
        return (x, swap(x, "segment"))

    small_p, mix_p, rate_p, inner_p, ow_p = both(small), both(mix), both(rate), both(inner), both(ow)
    sw_p, dn_p = both(sw), both(dn)
    att_w = small_p + mix_p + rate_p + inner_p + ow_p
    tok = (length, width)
    save_shapes = [
        ((length, wide), BF), ((2, 16), F32), ((length, 2 * wide), BF),
        ((length, heads * hid), BF), ((length, heads * hid), BF), ((length, heads * hid), BF),
        ((length, heads * hid), BF), ((length, heads * hid), BF), ((length, heads * hid), BF),
        ((10, length, wide), F32), ((length, 16), F32),
    ]
    sem = pltpu.SemaphoreType.DMA
    att_scratch = [
        pltpu.VMEM(mix.shape, BF), pltpu.VMEM(inner.shape, BF), pltpu.VMEM(small.shape, F32),
        pltpu.VMEM(rate.shape, BF), pltpu.VMEM(ow.shape, BF), sem((5,)),
    ]
    ffn_scratch = [pltpu.VMEM(small.shape, F32), pltpu.VMEM(sw.shape, BF), pltpu.VMEM(dn.shape, BF)]

    def ka(layer, ins):
        outs = [(tok, BF), (tok, BF), (tok, BF)] + save_shapes
        specs = [SMEM] + [VMEM] * (len(ins) - 1) + [ANY] * 10
        if layer == 1:
            outs = [(tok, BF)] + outs
        return call(functools.partial(ka_body, layer), f"mixer_fwd{layer}", list(ins) + list(att_w), specs, outs,
                    att_scratch, 6e9, 8e6)

    def exchange(x):
        return x, swap(x, "tensor")

    h0, x1_0, att, *save0 = ka(0, (dl, li))
    mixed0, stats0, save0 = save0[0], save0[1], save0[2:]
    ao, ar = exchange(att)
    h1_0, x2_0, hid_0, sl_0, si_0, fe = call(
        kf_body, "ffn_fwd0", [h0, ao, ar, *small_p, *sw_p, *dn_p], [VMEM] * 3 + [ANY] * 6,
        [(tok, F32), (tok, BF)] + [((length, ff), BF)] * 3 + [(tok, BF)], ffn_scratch + [sem((3,))], 1e9, 6e6)
    fo, fr = exchange(fe)
    lo0, hm, x1_1, att, *save1 = ka(1, (dl, h1_0, fo, fr))
    mixed1, stats1, save1 = save1[0], save1[1], save1[2:]
    ao, ar = exchange(att)
    pack_f = (length, 2 * width + ff + ff // 2)
    h1_1, fe, dxt, dfe1, keep, send = call(
        kfb_body, "ffn_both1", [dl, ct, hm, ao, ar, *small_p, *sw_p, *dn_p], [SMEM] + [VMEM] * 4 + [ANY] * 6,
        [(tok, F32), (tok, BF), (tok, BF), (tok, BF), (pack_f, BF), (pack_f, BF)],
        ffn_scratch + [sem((3,))], 2e9, 6e6)

    def grad_ffn(keep, send):
        recv = swap(send, "segment")
        return call(kgf_body, "grad_ffn", [keep, recv], [VMEM] * 2,
                    [((width, ff), BF), ((ff // 2, width), BF)], (), 1e9, 8e6)

    def grad_att(keep, send, ig):
        recv, other = swap(send, "segment"), swap(ig, "segment")
        return call(kga_body, "grad_mixer", [keep, recv, ig, other], [VMEM] * 4,
                    [((width, 2 * wide), BF), ((wide, width // 2), BF), ((INNER_ROWS // 2, hid), BF)], (), 1e9, 8e6)

    xo, xr = exchange(dxt)
    fo, fr = exchange(fe)
    pack_a = (length, width + 2 * wide + wide + width // 2)

    def kba(layer, xo, xr, dy, h1, x1, mixed, save):
        return call(functools.partial(kba_body, layer), f"mixer_bwd{layer}",
                    [dl, xo, xr, dy, h1, x1, mixed, *save, *att_w], [SMEM] + [VMEM] * 15 + [ANY] * 10,
                    [(tok, F32), (tok, BF), (pack_a, BF), (pack_a, BF), ((INNER_ROWS, hid), F32)],
                    att_scratch, 8e9, 8e6)

    dsw1, ddn1 = grad_ffn(keep, send)
    dh, dxo, keep, send, ig = kba(1, xo, xr, dfe1, h1_1, x1_1, mixed1, save1)
    dsw1, ddn1 = lax.psum((dsw1, ddn1), "dp")
    xo, xr = exchange(dxo)
    dmx1, dow1, din1 = grad_att(keep, send, ig)
    dmx1, dow1, din1 = lax.psum((dmx1, dow1, din1), "dp")
    ig1, gg1, dfe0, dxt, keep, send = call(
        kbf_body, "ffn_bwd0",
        [dl, hm, dh, xo, xr, *small_p, x2_0, hid_0, sl_0, si_0, *sw_p, *dn_p],
        [SMEM] + [VMEM] * 4 + [ANY] * 2 + [VMEM] * 4 + [ANY] * 4,
        [(tok, F32), ((1, width), F32), (tok, BF), (tok, BF), (pack_f, BF), (pack_f, BF)],
        ffn_scratch + [sem((1,)), sem((2,))], 1e9, 6e6)
    xo, xr = exchange(dxt)
    dsw0, ddn0 = grad_ffn(keep, send)
    dsw0, ddn0 = lax.psum((dsw0, ddn0), "dp")
    dh, dxo, keep, send, ig = kba(0, xo, xr, dfe0, h1_0, x1_0, mixed0, save0)
    xo, xr = exchange(dxo)
    dmx0, dow0, din0 = grad_att(keep, send, ig)
    dmx0, dow0, din0 = lax.psum((dmx0, dow0, din0), "dp")
    ig0, gg0 = call(ke_body, "input_grad0", [dl, h0, dh, xo, xr, *small_p], [SMEM] + [VMEM] * 4 + [ANY] * 2,
                    [(tok, F32), ((1, width), F32)], [pltpu.VMEM(small.shape, F32), sem((1,))], 1e6, 2e6)

    def lo1_body(dl_ref, h1_ref, fo_ref, fr_ref, lo_ref):
        begin, _ = doc_places(dl_ref, length // (2 * MBT))
        low = (h1_ref[...] + (fo_ref[...].astype(F32) + fr_ref[...].astype(F32))).astype(BF)
        scatter_rows(lo_ref, block_starts(begin, length // (2 * MBT)), low)

    (lo1,) = call(lo1_body, "output1", [dl, h1_1, fo, fr], [SMEM] + [VMEM] * 3, [(tok, BF)], (), 1e6, 2e6)

    def to_one(x):
        return lax.ppermute(x, "segment", [(0, 1)])

    def to_zero(x):
        return lax.ppermute(x, "segment", [(1, 0)])

    def two_rows(zero, one):
        return jnp.where(first, jnp.stack([zero, to_zero(zero)]), jnp.stack([to_one(one), one]))[None, :, None]

    def two_halves(zero, one):
        left = jnp.where(first, zero, to_one(one)).astype(F32)
        right = jnp.where(first, to_zero(zero), one).astype(F32)
        return left, right

    layer_output = two_rows(lo0, lo1)
    input_grads = two_rows(ig0, ig1)
    gains_zero = lax.psum(cat([gg0, gg1], 0), ("segment", "dp"))
    g_mix = cat(two_halves(dmx0, dmx1), 1).reshape(mixing.shape)
    g_out = cat(two_halves(dow0, dow1), 1)[None]
    g_sw = jnp.stack(two_halves(dsw0, dsw1), 1)[None]
    g_dn = cat(two_halves(ddn0, ddn1), 0)[None]
    g_in = cat(two_halves(din0, din1), 0)
    g_expand = g_in[: 64 * heads].reshape(expand.shape)
    g_contract = jnp.swapaxes(g_in[64 * heads : 128 * heads].reshape(1, heads, 64, hid), 2, 3)
    g_rate = cat([g_in[768 + heads * j : 768 + heads * (j + 1)] for j in range(3)], 1).T[None]
    g_hidden = g_in[786 : 786 + heads][None]
    tail = g_in[792:798].reshape(4, heads, 64)
    g_result, g_heads, g_shift = tail[0][None], tail[1:3][None], tail[3][None]
    g_offset = g_in[798, :heads][None]
    g_gain_two = g_in[799:802].reshape(-1)
    gain_one = jnp.where(first, gains_zero[0], gains_zero[1])
    g_gains = jnp.stack([gain_one, g_gain_two])[None]
    stats = jnp.stack([stats0, stats1])[:, :, :heads]
    gathered = lax.all_gather(stats, ("segment", "dp", "tensor"))
    dp = lax.axis_size("dp")
    gathered = gathered.reshape(micro, dp, 2, 2, 2, heads)
    picked = jnp.where(first, gathered[:, :, :, 0], gathered[:, :, :, 1])
    rate_stats = jnp.transpose(picked, (0, 1, 3, 2, 4)).reshape(1, micro, dp, 2, 2 * heads)
    return (
        layer_output, input_grads, g_gains, g_mix, g_rate, g_offset, g_expand, g_hidden, g_contract, g_result,
        g_heads, g_shift, g_out, g_sw, g_dn, rate_stats,
    )


def solution(mesh):
    placed = (
        P(None, "dp", None, None),
        P(None, "dp", None),
        P("segment", None, None),
        P("segment", None, None, "tensor"),
        P("segment", None, "tensor"),
        P("segment", "tensor"),
        P("segment", "tensor", None, None),
        P("segment", "tensor", None),
        P("segment", "tensor", None, None),
        P("segment", "tensor", None),
        P("segment", None, "tensor", None),
        P("segment", "tensor", None),
        P("segment", "tensor", None),
        P("segment", None, None, "tensor"),
        P("segment", "tensor", None),
        P(None, "dp", None, None),
    )
    return jax.shard_map(
        shards,
        mesh=mesh,
        in_specs=placed,
        out_specs=(
            P("segment", None, "dp", None, None),
            P("segment", None, "dp", None, None),
            P("segment", None, None),
            P("segment", None, None, "tensor"),
            P("segment", None, "tensor"),
            P("segment", "tensor"),
            P("segment", "tensor", None, None),
            P("segment", "tensor", None),
            P("segment", "tensor", None, None),
            P("segment", "tensor", None),
            P("segment", None, "tensor", None),
            P("segment", "tensor", None),
            P("segment", "tensor", None),
            P("segment", None, None, "tensor"),
            P("segment", "tensor", None),
            P("segment", None, None, None, None),
        ),
        check_vma=False,
    )
```

time: 2630 us -> 509 us (0.19); the launches traced: 2590 us -> 501 us
  matrix products: 609 us -> 0 us
  other arithmetic: 615 us -> 19.6 us
  local copies, waits for them, and re-layouts: 580 us -> 28.6 us
  waiting for transfers between devices: 696 us -> 193 us
  Pallas kernels: 0 us -> 91.9 us
  blocking collectives: 27.7 us -> 105 us
  starting transfers between devices: 8.37 us -> 47.4 us
  loops' own time: 34.8 us -> 0 us
    dot_general x1053 -> x0, matrix products: 609 us -> none  [the longest x1008 525 us: exact_dot(): return jnp.dot(left, right, precision=highest)]
    psum x13 -> x1, waiting for transfers between devices: 693 us -> 149 us  [shards(): dmx0, dow0, din0 = lax.psum((dmx0, dow0, din0), 'dp')]
    add x202 -> x0, other arithmetic: 196 us -> none  [the longest x96 95.8 us: block_update(): flag * start + (1.0 - flag) * now]
    squeeze x193 -> x0, local copies, waits for them, and re-layouts: 159 us -> none  [the longest x192 159 us: ttt_head(): lax.scan(jax.checkpoint(block_update), initial, (to_blocks(queries), to_b...]
    concatenate x1 -> x0, local copies, waits for them, and re-layouts: 139 us -> none  [flatten_all(): return jnp.concatenate([jnp.ravel(part) for part in parts])]
    reduce_sum x337 -> x0, other arithmetic: 97.6 us -> none  [the longest x48 29.2 us: block_update(): jnp.mean(misfit, axis=-1, keepdims=True)]
    pallas_call x0 -> x13, Pallas kernels: none -> 91.9 us  [call(): pl.pallas_call(body, out_shape=[jax.ShapeDtypeStruct(s, t) for s, t in ou...]
    sub x97 -> x0, other arithmetic: 79.7 us -> none  [the longest x24 31.1 us: block_update(): down_b - jnp.sum(step_two, axis=0)]
where the time goes in v1:
time: 509 us; the launch traced here: 501 us
  waiting for transfers between devices  193 us (38%)
  blocking collectives  105 us (21%)
  Pallas kernels  91.9 us (18%)
  starting transfers between devices  47.4 us (9%)
  local copies, waits for them, and re-layouts  28.6 us (6%)
  other arithmetic  19.6 us (4%)
  between operations  15.2 us (3%)
    psum x1, waiting for transfers between devices, shards(): dmx0, dow0, din0 = lax.psum((dmx0, dow0, din0), 'dp')  149 us
    pallas_call x13, Pallas kernels, call(): pl.pallas_call(body, out_shape=[jax.ShapeDtypeStruct(s, t) for s, t in ou...  91.9 us
    all_gather x1, blocking collectives, shards(): gathered = lax.all_gather(stats, ('segment', 'dp', 'tensor'))  73.8 us
    ppermute x21, waiting for transfers between devices, swap(): return lax.ppermute(value, axis, [(0, 1), (1, 0)])  44.6 us
    psum x1, blocking collectives, shards(): gains_zero = lax.psum(cat([gg0, gg1], 0), ('segment', 'dp'))  31.3 us
    ppermute x7, starting transfers between devices, to_one(): return lax.ppermute(x, 'segment', [(0, 1)])  23.7 us
    unnamed x93, local copies, waits for them, and re-layouts  21.5 us
    ppermute x21, starting transfers between devices, swap(): return lax.ppermute(value, axis, [(0, 1), (1, 0)])  14.5 us
  transfers between devices with their start and end apart: 36, of which 13 were waited for; matrix products, arithmetic and copies ran while one was open for 6% of the time, Pallas kernels for 8%

profile of v1, /device:TPU:0, one launch (start us, length us, event | category | flops | bytes accessed | tf_op | source)
XLA Modules:
  0.0 501.2 jit_solution(12333867812145779309)
XLA Ops:
  7.2 4.7 copy.63
  12.5 1.8 copy.62
  15.8 1.0 convert_bitcast_fusion.1
  16.9 0.9 collective-permute-done.args_3_.s_oth.args_5_.rest_10_.t_oth
  18.2 5.8 %collective-permute-done.2.args_7_.args_9_.rest_14_ = bf16[16,768]{1,0:T(8,128)(2,1)S(1)} collective-permute-done((bf16[16,768]{1,0:T(8,128)(2,1)S(1)}, bf16[16,768]{1,0:T(8,128)(2,1)S(1)}, u32[]{:S(2)}, u32[]{:S(2)}) %collective-permute-start.2) | collective-permute-done | bytes 24608 | tf_op jit(solution)/shard_map/ppermute | solution.py:752
  24.4 1.3 collective-permute-done.3.args_9_.args_11_.rest_16_
  25.8 15.1 %mixer_fwd0.1 = (bf16[128,768]{1,0:T(8,128)(2,1)S(1)}, bf16[128,768]{1,0:T(8,128)(2,1)S(1)}, bf16[128,768]{1,0:T(8,128)(2,1)S(1)}, bf16[128,384]{1,0:T(8,128)(2,...) custom-call(s32[2,3]{1,0:T(2,128)S(1)} %bitcast.86, ...), custom_call_target="tpu_custom_call" | custom-call | flops 6000000000 | bytes 8000000 | tf_op jit(solution)/shard_map/mixer_fwd0/pallas_call | solution.py:739
  42.4 2.9 collective-permute-start.5
  45.4 5.2 %collective-permute-done.5.ar_ref = bf16[128,768]{1,0:T(8,128)(2,1)S(1)} collective-permute-done((bf16[128,768]{1,0:T(8,128)(2,1)S(1)}, bf16[128,768]{1,0:T(8,128)(2,1)S(1)}, u32[]{:S(2)}, u32[]{:S(2)}) %collective-permute-start.5) | collective-permute-done | bytes 196640 | tf_op jit(solution)/shard_map/ppermute | solution.py:752
  50.6 3.1 ffn_fwd0.1
  53.7 1.8 collective-permute-start.8
  55.5 4.7 collective-permute-done.8.args_3_
  60.2 15.2 %mixer_fwd1.1 = (bf16[128,768]{1,0:T(8,128)(2,1)S(1)}, bf16[128,768]{1,0:T(8,128)(2,1)S(1)}, bf16[128,768]{1,0:T(8,128)(2,1)S(1)}, bf16[128,768]{1,0:T(8,128)(2,...) custom-call(s32[2,3]{1,0:T(2,128)S(1)} %bitcast.87, ...), custom_call_target="tpu_custom_call" | custom-call | flops 6000000000 | bytes 8000000 | tf_op jit(solution)/shard_map/mixer_fwd1/pallas_call | solution.py:739
  75.4 1.5 collective-permute-start.10
  76.9 4.2 collective-permute-done.10.ar_ref
  81.1 5.3 %ffn_both1.1 = (f32[128,768]{1,0:T(8,128)S(1)}, bf16[128,768]{1,0:T(8,128)(2,1)S(1)}, bf16[128,768]{1,0:T(8,128)(2,1)S(1)}, bf16[128,768]{1,0:T(8,128)(2,1)S(1)}...) custom-call(s32[2,3]{1,0:T(2,128)S(1)} %bitcast.88, bf16[2,128,768]{2,1,0:T(8,128)(2,1)S(1)} %bitcast.82, ...), custom_call_target="tpu_custom_call" | custom-call | flops 2000000000 | bytes 6000000 | tf_op jit(solution)/shard_map/ffn_both1/pallas_call | solution.py:739
  86.4 1.5 collective-permute-start.13
  87.9 4.2 collective-permute-done.13.xr_ref
  92.2 19.7 %mixer_bwd1.1 = (f32[128,768]{1,0:T(8,128)S(1)}, bf16[128,768]{1,0:T(8,128)(2,1)S(1)}, bf16[128,2304]{1,0:T(8,128)(2,1)S(1)}, bf16[128,2304]{1,0:T(8,128)(2,1)}, f32[832,256]{1,0:T(8,128)}) custom-call(s32[2,3]{1,0:T(2,128)S(1)} %bitcast.89, bf16[128,768]{1,0:T(8,128)(2,1)S(1)} %get-tuple-element.94.xo_ref, ...), custom_call_target="tpu_custom_call" | custom-call | flops 8000000000 | bytes 8000000 | tf_op jit(solution)/shard_map/mixer_bwd1/pallas_call | solution.py:739
  111.8 1.5 collective-permute-start.14
  113.3 4.2 collective-permute-done.14.xr_ref
  117.6 4.7 ffn_bwd0.1
  122.3 1.5 collective-permute-start.15
  124.3 3.7 collective-permute-done.15.xr_ref
  128.1 1.0 copy-done.22
  129.1 19.6 %mixer_bwd0.1 = (f32[128,768]{1,0:T(8,128)S(1)}, bf16[128,768]{1,0:T(8,128)(2,1)S(1)}, bf16[128,2304]{1,0:T(8,128)(2,1)S(1)}, bf16[128,2304]{1,0:T(8,128)(2,1)}, f32[832,256]{1,0:T(8,128)}) custom-call(s32[2,3]{1,0:T(2,128)S(1)} %bitcast.91, bf16[128,768]{1,0:T(8,128)(2,1)S(1)} %get-tuple-element.113.xo_ref, ...), custom_call_target="tpu_custom_call" | custom-call | flops 8000000000 | bytes 8000000 | tf_op jit(solution)/shard_map/mixer_bwd0/pallas_call | solution.py:739
  148.8 0.9 copy-done.9
  150.1 2.1 grad_ffn.3
  153.0 1.8 grad_mixer.3
  154.8 2.1 grad_ffn.2
  156.9 1.8 grad_mixer.2
  158.8 1.3 collective-permute-start.9
  160.1 73.8 %all-gather = f32[64,2,6]{2,1,0:T(2,128)S(1)} all-gather(f32[2,2,6]{2,1,0:T(2,128)S(1)} %pad_maximum_fusion.5), channel_id=2, replica_groups=mesh['segment'=2,'dp'=8,'tensor'=2] {'segment','dp','tensor'}, dimensions={0}, use_global_device_ids=true | all-gather | bytes 3168 | tf_op jit(solution)/shard_map/all_gather | solution.py:912
  234.1 6.5 %collective-permute-done.11.fr_ref = bf16[128,768]{1,0:T(8,128)(2,1)S(1)} collective-permute-done((bf16[128,768]{1,0:T(8,128)(2,1)S(1)}, bf16[128,768]{1,0:T(8,128)(2,1)S(1)}, u32[]{:S(2)}, u32[]{:S(2)}) %collective-permute-start.11) | collective-permute-done | bytes 196640 | tf_op jit(solution)/shard_map/ppermute | solution.py:752
  241.2 1.3 collective-permute-start.12
  243.7 2.0 collective-permute-start.18
  245.8 2.8 collective-permute-done.16.xr_ref
  248.6 0.9 input_grad0.1
  249.5 1.3 collective-permute-start.17
  251.6 31.3 %psum.77 = f32[2,768]{1,0:T(2,128)S(1)} all-reduce(f32[2,768]{1,0:T(2,128)S(1)} %pad_maximum_fusion.4), channel_id=1, replica_groups=mesh['segment'=2,'dp'=8,'tensor'=2] {'segment','dp'}, use_global_device_ids=true, to_apply=%region_0.1 | all-reduce | flops 1536 | bytes 12288 | tf_op jit(solution)/shard_map/psum | solution.py:895
  282.9 148.8 %all-reduce.5.cloned.1.call-done = (bf16[416,256]{1,0:T(8,128)(2,1)}, bf16[416,256]{1,0:T(8,128)(2,1)}, bf16[768,768]{1,0:T(8,128)(2,1)}, bf16[768,768]{1,0:T(8,...) async-done(((bf16[416,256]{1,0:T(8,128)(2,1)}, ...) | async-done | bytes 8093712 | tf_op jit(solution)/shard_map/psum | solution.py:868
  431.7 1.4 collective-permute-start.21
  433.1 2.0 maximum_select_fusion
  435.2 1.3 collective-permute-start.25
  436.5 5.2 %collective-permute-start.24 = (bf16[768,768]{1,0:T(8,128)(2,1)}, bf16[768,768]{1,0:T(8,128)(2,1)}, u32[]{:S(2)}, u32[]{:S(2)}) collective-permute-start(bf16[768,768]{1,0:T(8,128)(2,1)} %get-tuple-element.205), channel_id=1, source_target_pairs={{0,16},{1,17},{2,18},{3,19},{4,20},{5,21},{6,22},{7,23},{8,24},{9,... | collective-permute-start | bytes 3538952 | tf_op jit(solution)/shard_map/ppermute | solution.py:880
  441.6 1.3 collective-permute-start.26
  442.9 1.3 collective-permute-start.28
  444.3 4.5 collective-permute-start.27
  448.8 1.3 collective-permute-start.34
  450.2 0.9 pad_maximum_fusion
  455.3 4.1 collective-permute-start.33
  459.4 1.0 broadcast_select_fusion.4
  460.4 1.3 collective-permute-start.32
  461.7 1.0 broadcast_select_fusion.5
  462.7 1.1 fusion.2
  463.8 5.4 %collective-permute-start.31 = (bf16[768,1024]{1,0:T(8,128)(2,1)}, bf16[768,1024]{1,0:T(8,128)(2,1)}, u32[]{:S(2)}, u32[]{:S(2)}) collective-permute-start(bf16[768,1024]{1,0:T(8,128)(2,1)} %get-tuple-element.209), channel_id=1, source_target_pairs={{0,16},{1,17},{2,18},{3,19},{4,20},{5,21},{6,22},{7,23},{8,24},{9,... | collective-permute-start | bytes 4718600 | tf_op jit(solution)/shard_map/ppermute | solution.py:880
  469.2 1.2 broadcast_select_fusion.2
  470.4 1.2 broadcast_select_fusion.3
  471.7 1.9 fusion.1
  473.6 1.4 broadcast_select_fusion
  475.1 2.8 maximum_convert_fusion
  478.0 6.2 %reshape.209 = f32[1,768,4,384]{3,2,1,0:T(4,128)} reshape(f32[768,1536]{1,0:T(8,128)} %maximum_convert_fusion) | data formatting | bytes 9437184 | tf_op jit(solution)/shard_map/reshape | solution.py:896
  484.1 1.6 select_bitcast_fusion
  486.3 7.6 %copy.57 = f32[1,768,2,1024]{3,2,1,0:T(2,128)} copy(f32[1,768,2,1024]{3,1,2,0:T(8,128)S(1)} %fusion) | data formatting | bytes 12582912
  (161 shorter events, 14.2 us)
Async XLA Ops:
  7.2 424.5 %all-reduce.5.cloned.1.call-start = ((), (), s32[]{:S(2)}) async-start(), calls=%async_computation | async-start | bytes 16187392 | tf_op jit(solution)/shard_map/psum | solution.py:868
  7.2 5.2 %copy-start.25 = (bf16[1,768,4,384]{3,2,1,0:T(4,128)(2,1)S(1)}, bf16[1,768,4,384]{3,2,1,0:T(4,128)(2,1)}, u32[]{:S(2)}) copy-start(bf16[1,768,4,384]{3,2,1,0:T(4,128)(2,1)} %param.19) | copy-start | bytes 7077892
  12.0 38.6 %collective-permute-start.6 = (bf16[768,2048]{1,0:T(8,128)(2,1)}, bf16[768,2048]{1,0:T(8,128)(2,1)}, u32[]{:S(2)}, u32[]{:S(2)}) collective-permute-start(bf16[768,2048]{1,0:T(8,128)(2,1)} %bitcast.55.w_own), channel_id=1, source_target_pairs={{0,16},{16,0},{1,17},{17,1},{2,18},{18,2},{3,19},{19,3},{4,20},{20... | collective-permute-start | bytes 9437192 | tf_op jit(solution)/shard_map/ppermute | solution.py:752
  12.5 2.3 copy-start.34
  12.5 2.8 copy-start.6
  12.5 2.9 copy-start
  12.5 3.3 copy-start.29
  12.5 4.3 copy-start.32
  14.3 11.5 %copy-start.3 = (s32[2,1,3]{2,1,0:T(1,128)S(1)}, s32[2,1,3]{2,1,0:T(1,128)}, u32[]{:S(2)}) copy-start(s32[2,1,3]{2,1,0:T(1,128)} %param.17) | copy-start | bytes 76
  14.3 11.5 %copy-start.8 = (bf16[2,1,128,768]{3,2,1,0:T(8,128)(2,1)S(1)}, bf16[2,1,128,768]{3,2,1,0:T(8,128)(2,1)}, u32[]{:S(2)}) copy-start(bf16[2,1,128,768]{3,2,1,0:T(8,128)(2,1)} %param.16) | copy-start | bytes 1179652
  14.3 11.4 %collective-permute-start.1 = (bf16[768,1536]{1,0:T(8,128)(2,1)}, bf16[768,1536]{1,0:T(8,128)(2,1)}, u32[]{:S(2)}, u32[]{:S(2)}) collective-permute-start(bf16[768,1536]{1,0:T(8,128)(2,1)} %bitcast.52.args_4_.args_6_.rest_11_), channel_id=1, source_target_pairs={{0,16},{16,0},{1,17},{17,1},{2,18},{18,2},{3,19},{19,3},{4,20},{20... | collective-permute-start | bytes 7077896 | tf_op jit(solution)/shard_map/ppermute | solution.py:752
  14.8 3.0 collective-permute-start
  15.3 10.5 %collective-permute-start.4 = (bf16[384,768]{1,0:T(8,128)(2,1)S(1)}, bf16[384,768]{1,0:T(8,128)(2,1)S(1)}, u32[]{:S(2)}, u32[]{:S(2)}) collective-permute-start(bf16[384,768]{1,0:T(8,128)(2,1)S(1)} %bitcast.98), channel_id=1, source_target_pairs={{0,16},{16,0},{1,17},{17,1},{2,18},{18,2},{3,19},{19,3},{4,20},{20... | collective-permute-start | bytes 1769480 | tf_op jit(solution)/shard_map/ppermute | solution.py:752
  15.4 30.0 %collective-permute-start.7 = (bf16[1024,768]{1,0:T(8,128)(2,1)S(1)}, bf16[1024,768]{1,0:T(8,128)(2,1)S(1)}, u32[]{:S(2)}, u32[]{:S(2)}) collective-permute-start(bf16[1024,768]{1,0:T(8,128)(2,1)S(1)} %bitcast.77), channel_id=1, source_target_pairs={{0,16},{16,0},{1,17},{17,1},{2,18},{18,2},{3,19},{19,3},{4,20},{20... | collective-permute-start | bytes 4718600 | tf_op jit(solution)/shard_map/ppermute | solution.py:752
  17.8 6.3 %collective-permute-start.2 = (bf16[16,768]{1,0:T(8,128)(2,1)S(1)}, bf16[16,768]{1,0:T(8,128)(2,1)S(1)}, u32[]{:S(2)}, u32[]{:S(2)}) collective-permute-start(bf16[16,768]{1,0:T(8,128)(2,1)S(1)} %pad.9.args_6_.args_8_.rest_13_), channel_id=1, source_target_pairs={{0,16},{16,0},{1,17},{17,1},{2,18},{18,2},{3,19},{19,3},{4,20},{20... | collective-permute-start | bytes 73736 | tf_op jit(solution)/shard_map/ppermute | solution.py:752
  24.0 1.7 collective-permute-start.3
  25.8 15.1 %copy-start.7 = (bf16[384,768]{1,0:T(8,128)(2,1)}, bf16[384,768]{1,0:T(8,128)(2,1)S(1)}, u32[]{:S(2)}) copy-start(bf16[384,768]{1,0:T(8,128)(2,1)S(1)} %collective-permute-done.4.args_11_.args_13_.rest_18_) | copy-start | bytes 1769476
  42.4 11.3 %copy-start.15 = (bf16[128,1536]{1,0:T(8,128)(2,1)}, bf16[128,1536]{1,0:T(8,128)(2,1)S(1)}, u32[]{:S(2)}) copy-start(bf16[128,1536]{1,0:T(8,128)(2,1)S(1)} %get-tuple-element.120.rest_3_) | copy-start | bytes 1179652
  42.4 11.3 %copy-start.17 = (bf16[128,1536]{1,0:T(8,128)(2,1)}, bf16[128,1536]{1,0:T(8,128)(2,1)S(1)}, u32[]{:S(2)}) copy-start(bf16[128,1536]{1,0:T(8,128)(2,1)S(1)} %get-tuple-element.121.rest_4_) | copy-start | bytes 1179652
  42.4 11.3 %copy-start.19 = (bf16[128,1536]{1,0:T(8,128)(2,1)}, bf16[128,1536]{1,0:T(8,128)(2,1)S(1)}, u32[]{:S(2)}) copy-start(bf16[128,1536]{1,0:T(8,128)(2,1)S(1)} %get-tuple-element.122.rest_5_) | copy-start | bytes 1179652
  42.4 11.3 %copy-start.21 = (bf16[128,1536]{1,0:T(8,128)(2,1)}, bf16[128,1536]{1,0:T(8,128)(2,1)S(1)}, u32[]{:S(2)}) copy-start(bf16[128,1536]{1,0:T(8,128)(2,1)S(1)} %get-tuple-element.123.rest_6_) | copy-start | bytes 1179652
  42.4 11.3 %copy-start.23 = (bf16[128,768]{1,0:T(8,128)(2,1)}, bf16[128,768]{1,0:T(8,128)(2,1)S(1)}, u32[]{:S(2)}) copy-start(bf16[128,768]{1,0:T(8,128)(2,1)S(1)} %get-tuple-element.117.rest_0_) | copy-start | bytes 589828
  42.4 8.1 %collective-permute-start.5 = (bf16[128,768]{1,0:T(8,128)(2,1)S(1)}, bf16[128,768]{1,0:T(8,128)(2,1)S(1)}, u32[]{:S(2)}, u32[]{:S(2)}) collective-permute-start(bf16[128,768]{1,0:T(8,128)(2,1)S(1)} %get-tuple-element.86.ao_ref), channel_id=1, source_target_pairs={{0,1},{1,0},{2,3},{3,2},{4,5},{5,4},{6,7},{7,6},{8,9},{9,8},{10,11... | collective-permute-start | bytes 589832 | tf_op jit(solution)/shard_map/ppermute | solution.py:752
  45.3 8.4 %copy-start.1 = (bf16[1024,768]{1,0:T(8,128)(2,1)}, bf16[1024,768]{1,0:T(8,128)(2,1)S(1)}, u32[]{:S(2)}) copy-start(bf16[1024,768]{1,0:T(8,128)(2,1)S(1)} %collective-permute-done.7.d_oth) | copy-start | bytes 4718596
  53.7 6.5 %collective-permute-start.8 = (bf16[128,768]{1,0:T(8,128)(2,1)S(1)}, bf16[128,768]{1,0:T(8,128)(2,1)S(1)}, u32[]{:S(2)}, u32[]{:S(2)}) collective-permute-start(bf16[128,768]{1,0:T(8,128)(2,1)S(1)} %get-tuple-element.88.args_2_), channel_id=1, source_target_pairs={{0,1},{1,0},{2,3},{3,2},{4,5},{5,4},{6,7},{7,6},{8,9},{9,8},{10,11... | collective-permute-start | bytes 589832 | tf_op jit(solution)/shard_map/ppermute | solution.py:752
  60.2 20.9 %copy-start.2 = (bf16[2,1,128,768]{3,2,1,0:T(8,128)(2,1)S(1)}, bf16[2,1,128,768]{3,2,1,0:T(8,128)(2,1)}, u32[]{:S(2)}) copy-start(bf16[2,1,128,768]{3,2,1,0:T(8,128)(2,1)} %param.31) | copy-start | bytes 1179652
  75.4 5.7 %collective-permute-start.10 = (bf16[128,768]{1,0:T(8,128)(2,1)S(1)}, bf16[128,768]{1,0:T(8,128)(2,1)S(1)}, u32[]{:S(2)}, u32[]{:S(2)}) collective-permute-start(bf16[128,768]{1,0:T(8,128)(2,1)S(1)} %get-tuple-element.91.ao_ref), channel_id=1, source_target_pairs={{0,1},{1,0},{2,3},{3,2},{4,5},{5,4},{6,7},{7,6},{8,9},{9,8},{10,11... | collective-permute-start | bytes 589832 | tf_op jit(solution)/shard_map/ppermute | solution.py:752
  86.4 5.7 %collective-permute-start.13 = (bf16[128,768]{1,0:T(8,128)(2,1)S(1)}, bf16[128,768]{1,0:T(8,128)(2,1)S(1)}, u32[]{:S(2)}, u32[]{:S(2)}) collective-permute-start(bf16[128,768]{1,0:T(8,128)(2,1)S(1)} %get-tuple-element.94.xo_ref), channel_id=1, source_target_pairs={{0,1},{1,0},{2,3},{3,2},{4,5},{5,4},{6,7},{7,6},{8,9},{9,8},{10,11... | collective-permute-start | bytes 589832 | tf_op jit(solution)/shard_map/ppermute | solution.py:752
  111.8 5.7 %collective-permute-start.14 = (bf16[128,768]{1,0:T(8,128)(2,1)S(1)}, bf16[128,768]{1,0:T(8,128)(2,1)S(1)}, u32[]{:S(2)}, u32[]{:S(2)}) collective-permute-start(bf16[128,768]{1,0:T(8,128)(2,1)S(1)} %get-tuple-element.108.xo_ref), channel_id=1, source_target_pairs={{0,1},{1,0},{2,3},{3,2},{4,5},{5,4},{6,7},{7,6},{8,9},{9,8},{10,11... | collective-permute-start | bytes 589832 | tf_op jit(solution)/shard_map/ppermute | solution.py:752
  117.6 6.2 %copy-start.4 = (f32[832,256]{1,0:T(8,128)S(1)}, f32[832,256]{1,0:T(8,128)}, u32[]{:S(2)}) copy-start(f32[832,256]{1,0:T(8,128)} %get-tuple-element.138.ik_ref) | copy-start | bytes 2555908
  117.6 10.5 %copy-start.12 = (bf16[128,1536]{1,0:T(8,128)(2,1)S(1)}, bf16[128,1536]{1,0:T(8,128)(2,1)}, u32[]{:S(2)}) copy-start(bf16[128,1536]{1,0:T(8,128)(2,1)} %copy-done.11) | copy-start | bytes 1179652
  117.6 10.5 %copy-start.14 = (bf16[128,1536]{1,0:T(8,128)(2,1)S(1)}, bf16[128,1536]{1,0:T(8,128)(2,1)}, u32[]{:S(2)}) copy-start(bf16[128,1536]{1,0:T(8,128)(2,1)} %copy-done.13) | copy-start | bytes 1179652
  117.6 10.5 %copy-start.16 = (bf16[128,1536]{1,0:T(8,128)(2,1)S(1)}, bf16[128,1536]{1,0:T(8,128)(2,1)}, u32[]{:S(2)}) copy-start(bf16[128,1536]{1,0:T(8,128)(2,1)} %copy-done.15) | copy-start | bytes 1179652
  117.6 10.5 %copy-start.18 = (bf16[128,1536]{1,0:T(8,128)(2,1)S(1)}, bf16[128,1536]{1,0:T(8,128)(2,1)}, u32[]{:S(2)}) copy-start(bf16[128,1536]{1,0:T(8,128)(2,1)} %copy-done.17) | copy-start | bytes 1179652
  117.6 10.5 %copy-start.20 = (bf16[128,1536]{1,0:T(8,128)(2,1)S(1)}, bf16[128,1536]{1,0:T(8,128)(2,1)}, u32[]{:S(2)}) copy-start(bf16[128,1536]{1,0:T(8,128)(2,1)} %copy-done.19) | copy-start | bytes 1179652
  117.6 10.5 %copy-start.24 = (bf16[128,768]{1,0:T(8,128)(2,1)S(1)}, bf16[128,768]{1,0:T(8,128)(2,1)}, u32[]{:S(2)}) copy-start(bf16[128,768]{1,0:T(8,128)(2,1)} %copy-done.23) | copy-start | bytes 589828
  122.3 5.7 %collective-permute-start.15 = (bf16[128,768]{1,0:T(8,128)(2,1)S(1)}, bf16[128,768]{1,0:T(8,128)(2,1)S(1)}, u32[]{:S(2)}, u32[]{:S(2)}) collective-permute-start(bf16[128,768]{1,0:T(8,128)(2,1)S(1)} %get-tuple-element.113.xo_ref), channel_id=1, source_target_pairs={{0,1},{1,0},{2,3},{3,2},{4,5},{5,4},{6,7},{7,6},{8,9},{9,8},{10,11... | collective-permute-start | bytes 589832 | tf_op jit(solution)/shard_map/ppermute | solution.py:752
  123.8 26.3 %collective-permute-start.30 = (bf16[128,3072]{1,0:T(8,128)(2,1)S(1)}, bf16[128,3072]{1,0:T(8,128)(2,1)S(1)}, u32[]{:S(2)}, u32[]{:S(2)}) collective-permute-start(bf16[128,3072]{1,0:T(8,128)(2,1)S(1)} %get-tuple-element.148), channel_id=1, source_target_pairs={{0,16},{16,0},{1,17},{17,1},{2,18},{18,2},{3,19},{19,3},{4,20},{20... | collective-permute-start | bytes 2359304 | tf_op jit(solution)/shard_map/ppermute | solution.py:752
  123.8 29.2 %collective-permute-start.23 = (f32[832,256]{1,0:T(8,128)S(1)}, f32[832,256]{1,0:T(8,128)S(1)}, u32[]{:S(2)}, u32[]{:S(2)}) collective-permute-start(f32[832,256]{1,0:T(8,128)S(1)} %copy-done.4), channel_id=1, source_target_pairs={{0,16},{16,0},{1,17},{17,1},{2,18},{18,2},{3,19},{19,3},{4,20},{20... | collective-permute-start | bytes 2555912 | tf_op jit(solution)/shard_map/ppermute | solution.py:752
  124.3 30.5 %collective-permute-start.29 = (bf16[128,3072]{1,0:T(8,128)(2,1)S(1)}, bf16[128,3072]{1,0:T(8,128)(2,1)S(1)}, u32[]{:S(2)}, u32[]{:S(2)}) collective-permute-start(bf16[128,3072]{1,0:T(8,128)(2,1)S(1)} %get-tuple-element.145), channel_id=1, source_target_pairs={{0,16},{16,0},{1,17},{17,1},{2,18},{18,2},{3,19},{19,3},{4,20},{20... | collective-permute-start | bytes 2359304 | tf_op jit(solution)/shard_map/ppermute | solution.py:752
  149.6 7.3 %collective-permute-start.20 = (f32[832,256]{1,0:T(8,128)}, f32[832,256]{1,0:T(8,128)S(1)}, u32[]{:S(2)}, u32[]{:S(2)}) collective-permute-start(f32[832,256]{1,0:T(8,128)} %get-tuple-element.134.ik_ref), channel_id=1, source_target_pairs={{0,16},{16,0},{1,17},{17,1},{2,18},{18,2},{3,19},{19,3},{4,20},{20... | collective-permute-start | bytes 2555912 | tf_op jit(solution)/shard_map/ppermute | solution.py:752
  149.6 3.4 collective-permute-start.22
  150.1 6.8 %collective-permute-start.19 = (bf16[128,2304]{1,0:T(8,128)(2,1)}, bf16[128,2304]{1,0:T(8,128)(2,1)S(1)}, u32[]{:S(2)}, u32[]{:S(2)}) collective-permute-start(bf16[128,2304]{1,0:T(8,128)(2,1)} %get-tuple-element.133), channel_id=1, source_target_pairs={{0,16},{16,0},{1,17},{17,1},{2,18},{18,2},{3,19},{19,3},{4,20},{20... | collective-permute-start | bytes 1769480 | tf_op jit(solution)/shard_map/ppermute | solution.py:752
  158.8 92.0 %collective-permute-start.9 = (bf16[128,768]{1,0:T(8,128)(2,1)S(1)}, bf16[128,768]{1,0:T(8,128)(2,1)S(1)}, u32[]{:S(2)}, u32[]{:S(2)}) collective-permute-start(bf16[128,768]{1,0:T(8,128)(2,1)S(1)} %get-tuple-element.89), channel_id=1, source_target_pairs={{16,0},{17,1},{18,2},{19,3},{20,4},{21,5},{22,6},{23,7},{24,8},{25... | collective-permute-start | bytes 589832 | tf_op jit(solution)/shard_map/ppermute | solution.py:883
  233.8 6.8 %collective-permute-start.11 = (bf16[128,768]{1,0:T(8,128)(2,1)S(1)}, bf16[128,768]{1,0:T(8,128)(2,1)S(1)}, u32[]{:S(2)}, u32[]{:S(2)}) collective-permute-start(bf16[128,768]{1,0:T(8,128)(2,1)S(1)} %get-tuple-element.93.fo_ref), channel_id=1, source_target_pairs={{0,1},{1,0},{2,3},{3,2},{4,5},{5,4},{6,7},{7,6},{8,9},{9,8},{10,11... | collective-permute-start | bytes 589832 | tf_op jit(solution)/shard_map/ppermute | solution.py:752
  241.2 9.6 %collective-permute-start.12 = (bf16[128,768]{1,0:T(8,128)(2,1)S(1)}, bf16[128,768]{1,0:T(8,128)(2,1)S(1)}, u32[]{:S(2)}, u32[]{:S(2)}) collective-permute-start(bf16[128,768]{1,0:T(8,128)(2,1)S(1)} %output1.1), channel_id=1, source_target_pairs={{0,16},{1,17},{2,18},{3,19},{4,20},{5,21},{6,22},{7,23},{8,24},{9,... | collective-permute-start | bytes 589832 | tf_op jit(solution)/shard_map/ppermute | solution.py:880
  242.5 6.1 %collective-permute-start.16 = (bf16[128,768]{1,0:T(8,128)(2,1)S(1)}, bf16[128,768]{1,0:T(8,128)(2,1)S(1)}, u32[]{:S(2)}, u32[]{:S(2)}) collective-permute-start(bf16[128,768]{1,0:T(8,128)(2,1)S(1)} %get-tuple-element.127.xo_ref), channel_id=1, source_target_pairs={{0,1},{1,0},{2,3},{3,2},{4,5},{5,4},{6,7},{7,6},{8,9},{9,8},{10,11... | collective-permute-start | bytes 589832 | tf_op jit(solution)/shard_map/ppermute | solution.py:752
  243.7 189.4 %collective-permute-start.18 = (f32[128,768]{1,0:T(8,128)S(1)}, f32[128,768]{1,0:T(8,128)}, u32[]{:S(2)}, u32[]{:S(2)}) collective-permute-start(f32[128,768]{1,0:T(8,128)S(1)} %get-tuple-element.129), channel_id=1, source_target_pairs={{0,16},{1,17},{2,18},{3,19},{4,20},{5,21},{6,22},{7,23},{8,24},{9,... | collective-permute-start | bytes 1179656 | tf_op jit(solution)/shard_map/ppermute | solution.py:880
  249.5 183.6 %collective-permute-start.17 = (f32[128,768]{1,0:T(8,128)S(1)}, f32[128,768]{1,0:T(8,128)S(1)}, u32[]{:S(2)}, u32[]{:S(2)}) collective-permute-start(f32[128,768]{1,0:T(8,128)S(1)} %get-tuple-element.128), channel_id=1, source_target_pairs={{16,0},{17,1},{18,2},{19,3},{20,4},{21,5},{22,6},{23,7},{24,8},{25... | collective-permute-start | bytes 1179656 | tf_op jit(solution)/shard_map/ppermute | solution.py:883
  431.7 3.5 copy-start.27
  431.7 10.0 %copy-start.31 = (bf16[416,256]{1,0:T(8,128)(2,1)S(1)}, bf16[416,256]{1,0:T(8,128)(2,1)}, u32[]{:S(2)}) copy-start(bf16[416,256]{1,0:T(8,128)(2,1)} %get-tuple-element.203) | copy-start | bytes 638980
  431.7 12.6 %collective-permute-start.21 = (bf16[416,256]{1,0:T(8,128)(2,1)}, bf16[416,256]{1,0:T(8,128)(2,1)S(1)}, u32[]{:S(2)}, u32[]{:S(2)}) collective-permute-start(bf16[416,256]{1,0:T(8,128)(2,1)} %get-tuple-element.202), channel_id=1, source_target_pairs={{16,0},{17,1},{18,2},{19,3},{20,4},{21,5},{22,6},{23,7},{24,8},{25... | collective-permute-start | bytes 638984 | tf_op jit(solution)/shard_map/ppermute | solution.py:883
  433.1 17.0 %copy-start.30 = (bf16[416,256]{1,0:T(8,128)(2,1)S(1)}, bf16[416,256]{1,0:T(8,128)(2,1)}, u32[]{:S(2)}) copy-start(bf16[416,256]{1,0:T(8,128)(2,1)} %get-tuple-element.202) | copy-start | bytes 638980
  435.2 38.4 %collective-permute-start.25 = (bf16[768,768]{1,0:T(8,128)(2,1)S(1)}, bf16[768,768]{1,0:T(8,128)(2,1)}, u32[]{:S(2)}, u32[]{:S(2)}) collective-permute-start(bf16[768,768]{1,0:T(8,128)(2,1)S(1)} %copy-done.27), channel_id=1, source_target_pairs={{16,0},{17,1},{18,2},{19,3},{20,4},{21,5},{22,6},{23,7},{24,8},{25... | collective-permute-start | bytes 3538952 | tf_op jit(solution)/shard_map/ppermute | solution.py:883
  436.5 38.5 %collective-permute-start.24 = (bf16[768,768]{1,0:T(8,128)(2,1)}, bf16[768,768]{1,0:T(8,128)(2,1)}, u32[]{:S(2)}, u32[]{:S(2)}) collective-permute-start(bf16[768,768]{1,0:T(8,128)(2,1)} %get-tuple-element.205), channel_id=1, source_target_pairs={{0,16},{1,17},{2,18},{3,19},{4,20},{5,21},{6,22},{7,23},{8,24},{9,... | collective-permute-start | bytes 3538952 | tf_op jit(solution)/shard_map/ppermute | solution.py:880
  441.6 7.2 %collective-permute-start.26 = (bf16[416,256]{1,0:T(8,128)(2,1)S(1)}, bf16[416,256]{1,0:T(8,128)(2,1)S(1)}, u32[]{:S(2)}, u32[]{:S(2)}) collective-permute-start(bf16[416,256]{1,0:T(8,128)(2,1)S(1)} %copy-done.31), channel_id=1, source_target_pairs={{0,16},{1,17},{2,18},{3,19},{4,20},{5,21},{6,22},{7,23},{8,24},{9,... | collective-permute-start | bytes 638984 | tf_op jit(solution)/shard_map/ppermute | solution.py:880
  442.9 12.4 %collective-permute-start.28 = (bf16[384,384]{1,0:T(8,128)(2,1)}, bf16[384,384]{1,0:T(8,128)(2,1)}, u32[]{:S(2)}, u32[]{:S(2)}) collective-permute-start(bf16[384,384]{1,0:T(8,128)(2,1)} %get-tuple-element.206), channel_id=1, source_target_pairs={{16,0},{17,1},{18,2},{19,3},{20,4},{21,5},{22,6},{23,7},{24,8},{25... | collective-permute-start | bytes 884744 | tf_op jit(solution)/shard_map/ppermute | solution.py:883
  444.3 16.1 %collective-permute-start.27 = (bf16[384,384]{1,0:T(8,128)(2,1)}, bf16[384,384]{1,0:T(8,128)(2,1)}, u32[]{:S(2)}, u32[]{:S(2)}) collective-permute-start(bf16[384,384]{1,0:T(8,128)(2,1)} %get-tuple-element.207), channel_id=1, source_target_pairs={{0,16},{1,17},{2,18},{3,19},{4,20},{5,21},{6,22},{7,23},{8,24},{9,... | collective-permute-start | bytes 884744 | tf_op jit(solution)/shard_map/ppermute | solution.py:880
  448.8 15.0 %collective-permute-start.34 = (bf16[512,768]{1,0:T(8,128)(2,1)}, bf16[512,768]{1,0:T(8,128)(2,1)}, u32[]{:S(2)}, u32[]{:S(2)}) collective-permute-start(bf16[512,768]{1,0:T(8,128)(2,1)} %get-tuple-element.210), channel_id=1, source_target_pairs={{16,0},{17,1},{18,2},{19,3},{20,4},{21,5},{22,6},{23,7},{24,8},{25... | collective-permute-start | bytes 2359304 | tf_op jit(solution)/shard_map/ppermute | solution.py:883
  450.2 10.2 %copy-start.26 = (bf16[768,1024]{1,0:T(8,128)(2,1)S(1)}, bf16[768,1024]{1,0:T(8,128)(2,1)}, u32[]{:S(2)}) copy-start(bf16[768,1024]{1,0:T(8,128)(2,1)} %get-tuple-element.208) | copy-start | bytes 4718596
  455.3 13.9 %copy-start.28 = (bf16[512,768]{1,0:T(8,128)(2,1)S(1)}, bf16[512,768]{1,0:T(8,128)(2,1)}, u32[]{:S(2)}) copy-start(bf16[512,768]{1,0:T(8,128)(2,1)} %get-tuple-element.211) | copy-start | bytes 2359300
  455.3 15.1 %collective-permute-start.33 = (bf16[512,768]{1,0:T(8,128)(2,1)}, bf16[512,768]{1,0:T(8,128)(2,1)S(1)}, u32[]{:S(2)}, u32[]{:S(2)}) collective-permute-start(bf16[512,768]{1,0:T(8,128)(2,1)} %get-tuple-element.211), channel_id=1, source_target_pairs={{0,16},{1,17},{2,18},{3,19},{4,20},{5,21},{6,22},{7,23},{8,24},{9,... | collective-permute-start | bytes 2359304 | tf_op jit(solution)/shard_map/ppermute | solution.py:880
  460.4 23.7 %collective-permute-start.32 = (bf16[768,1024]{1,0:T(8,128)(2,1)S(1)}, bf16[768,1024]{1,0:T(8,128)(2,1)}, u32[]{:S(2)}, u32[]{:S(2)}) collective-permute-start(bf16[768,1024]{1,0:T(8,128)(2,1)S(1)} %copy-done.26), channel_id=1, source_target_pairs={{16,0},{17,1},{18,2},{19,3},{20,4},{21,5},{22,6},{23,7},{24,8},{25... | collective-permute-start | bytes 4718600 | tf_op jit(solution)/shard_map/ppermute | solution.py:883
  463.8 21.9 %collective-permute-start.31 = (bf16[768,1024]{1,0:T(8,128)(2,1)}, bf16[768,1024]{1,0:T(8,128)(2,1)}, u32[]{:S(2)}, u32[]{:S(2)}) collective-permute-start(bf16[768,1024]{1,0:T(8,128)(2,1)} %get-tuple-element.209), channel_id=1, source_target_pairs={{0,16},{1,17},{2,18},{3,19},{4,20},{5,21},{6,22},{7,23},{8,24},{9,... | collective-permute-start | bytes 4718600 | tf_op jit(solution)/shard_map/ppermute | solution.py:880
  (11 other events, 18.0 us)
Sparse Core Ops, SparseCore 0:
  158.9 272.7 all-reduce.4
